TPU v7x, 128 devices: a whole 4x4x4 slice. The times are simulated.
128 devices in a mesh: dp: 16 (over z, x), tensor: 8 (over y, core).
Axes of the slice: x: 4, y: 4, z: 4, core: 2. Of those that a mesh axis runs over, the one named last changes fastest.
Arguments:
- tokens_in: bfloat16 [8192, 4096], P('dp'), may hold values from -6 to 6
- teacher_hidden: bfloat16 [8192, 12288], P('dp', 'tensor'), may hold values from -6 to 6
- up_old: bfloat16 [6144, 12288], P('dp', 'tensor'), may hold values from -0.09375 to 0.09375
- gain_old: float32 [6144], replicated, may hold values from 0.25 to 1.75
- keep_chan: int32 [4096], replicated, may hold values from 0 to 6143, as said below
- keep_ff: int32 [8192], replicated, may hold values from 0 to 12287, as said below
Outputs:
- grad_up: float32 [4096, 8192], P('dp', 'tensor')
Inputs may be any that keep to these rules, and one draw needn't show every extreme that they name: Distinct old hidden units. Entry j has new owner j // 1024 and old owner keep_ff[j] // 1536; at most 256 entries of one new owner have one old owner, and some pair reaches it. Each new owner takes entries from every old owner but one. Every old owner has exactly 1024 entries in all. `keep_chan`: distinct old channels. At most 320 entries lie in one aligned block of 384 old channels, and some block reaches it.
All inputs are finite; a program needn't handle non-finite values.
Results may differ from a plain program's by a relative error of at most 0.019.
Values may be sent and summed in bfloat16 or wider, within the bound.
A program may use at most 128 MiB of HBM per device.

v0:
```python
import math

import jax
import jax.numpy as jnp
from jax import lax
from jax.sharding import PartitionSpec as P


def rank_within(source, groups):
    hits = (source[:, None] == jnp.arange(groups, dtype=jnp.int32)[None, :]).astype(jnp.int32)
    return jnp.sum((jnp.cumsum(hits, axis=0) - 1) * hits, axis=1)


def pick_columns(matrix, index, width):
    table = (jnp.arange(width, dtype=jnp.int32)[:, None] == index[None, :]).astype(jnp.bfloat16)
    return jnp.dot(matrix, table, preferred_element_type=jnp.float32).astype(jnp.bfloat16)


def kept_matrix(weight_cols, keep_chan):
    gathered = lax.all_gather(weight_cols, "dp", axis=0, tiled=True)
    return jnp.take(gathered, keep_chan, axis=0)


def per_device(tokens_in, teacher_hidden, up_old, gain_old, keep_chan, keep_ff):
    tensor_count = lax.axis_size("tensor")
    data_count = lax.axis_size("dp")
    owner = lax.axis_index("tensor")
    old_width = up_old.shape[1]
    new_width = keep_ff.shape[0] // tensor_count
    slots = 2 * new_width // tensor_count
    blocks_ff = keep_ff.reshape(tensor_count, new_width)
    mine = blocks_ff // old_width == owner
    ranks = jnp.cumsum(mine.astype(jnp.int32), axis=1) - 1
    own_cols = lax.dynamic_slice_in_dim(keep_ff, owner * new_width, new_width)
    source = own_cols // old_width
    where_from = source * slots + rank_within(source, tensor_count)
    gain = jnp.take(gain_old, keep_chan)
    values = tokens_in.astype(jnp.float32)
    center = jnp.mean(values, axis=1, keepdims=True)
    spread = jnp.mean((values - center) ** 2, axis=1, keepdims=True)
    normed = ((values - center) * lax.rsqrt(spread + 1e-05) * gain).astype(jnp.bfloat16)
    scale = 1.0 / math.sqrt(tokens_in.shape[0] * data_count)
    targets_row = jnp.broadcast_to(
        jnp.arange(tensor_count, dtype=jnp.int32)[:, None], (tensor_count, new_width)
    )
    columns = (
        jnp.zeros((tensor_count, slots), jnp.int32)
        .at[targets_row, jnp.where(mine, ranks, slots)]
        .set(blocks_ff % old_width, mode="drop")
        .reshape(-1)
    )
    packed_weight = pick_columns(up_old, columns, old_width)
    packed_target = pick_columns(teacher_hidden, columns, old_width)
    got_weight, got_target = (
        lax.all_to_all(packed_weight, "tensor", split_axis=1, concat_axis=1, tiled=True),
        lax.all_to_all(packed_target, "tensor", split_axis=1, concat_axis=1, tiled=True),
    )
    received = tensor_count * slots
    weight_cols = pick_columns(got_weight, where_from, received)
    target = pick_columns(got_target, where_from, received)
    pre = jnp.dot(normed, kept_matrix(weight_cols, keep_chan), preferred_element_type=jnp.float32)
    active = jnp.maximum(pre, 0.0)
    delta = (2.0 * active * (active * active - target.astype(jnp.float32)) * scale).astype(
        jnp.bfloat16
    )
    return lax.psum_scatter(
        lax.dot_general(
            normed, delta, (((0,), (0,)), ((), ())), preferred_element_type=jnp.float32
        ).astype(jnp.bfloat16),
        "dp",
        scatter_dimension=0,
        tiled=True,
    ).astype(jnp.float32)


def solution(mesh):
    return jax.shard_map(
        per_device,
        mesh=mesh,
        in_specs=(P("dp", None), P("dp", "tensor"), P("dp", "tensor"), P(), P(), P()),
        out_specs=P("dp", "tensor"),
        check_vma=False,
    )
```

profile of v0, /device:TPU:34, one launch (start us, length us, event | category | flops | bytes accessed | tf_op | source)
XLA Modules:
  0.0 305.0 jit_solution(9256960772796768558)
XLA Ops:
  6.5 0.0 copy-start
  6.5 0.9 broadcast_remainder_fusion
  7.4 0.8 fusion.37
  8.2 2.3 reduce-window.14
  10.5 0.3 slice_reduce_fusion.1
  10.8 0.2 reduce-window.15
  10.9 0.1 add_add_fusion
  11.1 0.7 multiply_reduce_fusion
  11.9 0.7 and_reduce_fusion
  12.7 30.4 %scatter_custom_fusion = s32[2048]{0:T(1024)S(1)} fusion(s32[8192]{0:T(1024)S(1)} %get-tuple-element.12, s32[8192]{0:T(1024)S(1)} %get-tuple-element.11, s32[]{:T(128)} %constant.54.clone.1), kind=kCustom, calls=%fused_computation.64 | custom fusion | bytes 8196
  43.1 5.9 %fusion.23 = bf16[2048,384]{1,0:T(8,128)(2,1)} fusion(bf16[384,1536]{1,0:T(8,128)(2,1)} %param.8, s32[2048]{0:T(1024)S(1)} %scatter_custom_fusion), kind=kOutput, calls=%fused_computation.27 | convolution fusion | flops 2422996992 | bytes 2760704 | tf_op jit(solution)/shard_map/dot_general | solution.py:16
  49.0 4.5 %all-to-all-start = ((bf16[384,8,256]{0,2,1:T(8,128)(2,1)}), bf16[384,8,256]{0,2,1:T(8,128)(2,1)S(1)}, u32[]{:S(2)}, u32[]{:S(2)}) async-start(bf16[384,8,256]{0,2,1:T(8,128)(2,1)} %bitcast.47), calls=%async_computation | async-start | bytes 3145728 | tf_op jit(solution)/shard_map/all_to_all | solution.py:55
  53.5 0.0 all-gather.2.cloned.1.call-start
  53.5 0.7 fusion.51
  54.2 2.3 reduce-window.16
  56.5 0.3 slice_reduce_fusion
  56.8 0.2 reduce-window.19
  56.9 0.7 add_select_fusion.3
  57.6 0.1 add_bitcast_fusion
  57.7 0.7 multiply_add_fusion
  58.5 16.6 %all-to-all-done = bf16[384,8,256]{0,2,1:T(8,128)(2,1)S(1)} async-done(((bf16[384,8,256]{0,2,1:T(8,128)(2,1)}), bf16[384,8,256]{0,2,1:T(8,128)(2,1)S(1)}, u32[]{:S(2)}, u32[]{:S(2)}) %all-to-all-start) | async-done | bytes 1572896 | tf_op jit(solution)/shard_map/all_to_all | solution.py:55
  75.1 2.8 fusion.29
  77.8 0.0 all-gather.2.cloned.1.call-update
  77.8 0.0 copy-done
  77.9 4.7 %fusion.20 = bf16[2048,512]{1,0:T(8,128)(2,1)} fusion(bf16[512,1536]{1,0:T(8,128)(2,1)S(1)} %copy-done, s32[2048]{0:T(1024)S(1)} %scatter_custom_fusion), kind=kOutput, calls=%fused_computation.26 | convolution fusion | flops 3228565504 | bytes 3678208 | tf_op jit(solution)/shard_map/dot_general | solution.py:16
  82.6 0.0 copy-start.4
  82.6 0.0 copy-start.1
  82.6 4.5 %all-to-all-start.1 = ((bf16[512,8,256]{0,2,1:T(8,128)(2,1)}), bf16[512,8,256]{0,2,1:T(8,128)(2,1)}, u32[]{:S(2)}, u32[]{:S(2)}) async-start(bf16[512,8,256]{0,2,1:T(8,128)(2,1)} %bitcast.45), calls=%async_computation.1 | async-start | bytes 4194304 | tf_op jit(solution)/shard_map/all_to_all | solution.py:56
  87.1 0.2 reduce-scatter.2.cloned.1.call-start
  87.3 0.0 copy-done.4
  87.3 0.0 copy-done.1
  87.3 23.0 %gather_fusion = f32[4096]{0:T(1024)S(1)} fusion(f32[6144]{0:T(1024)S(1)} %copy-done.1, s32[4096]{0:T(1024)S(1)} %fusion.38), kind=kCustom, calls=%fused_computation | custom fusion | bytes 49152 | tf_op jit(solution)/shard_map/jit(_take)/gather | solution.py:37
  110.4 0.0 copy-start.2
  110.4 3.0 convert_reduce_fusion
  113.4 0.5 copy-done.2
  113.8 1.2 fusion.7
  115.1 0.0 all-to-all-done.1
  115.1 4.1 %fusion.28 = bf16[512,1024]{1,0:T(8,128)(2,1)S(1)} fusion(bf16[512,2048]{0,1:T(8,128)(2,1)} %bitcast.9, s32[1024]{0:T(1024)S(1)} %multiply_add_fusion), kind=kOutput, calls=%fused_computation.29 | convolution fusion | flops 2150105088 | bytes 3149824 | tf_op jit(solution)/shard_map/dot_general | solution.py:16
  119.2 47.6 %all-gather.2.cloned.1.call-done = bf16[6144,1024]{1,0:T(8,128)(2,1)} async-done(((bf16[384,1024]{1,0:T(8,128)(2,1)}), bf16[6144,1024]{1,0:T(8,128)(2,1)}) %all-gather.2.cloned.1.call-update) | async-done | bytes 12582928 | tf_op jit(solution)/shard_map/all_gather | solution.py:20
  166.7 27.1 %gather_fusion.1 = bf16[4096,1024]{1,0:T(8,128)(2,1)} fusion(bf16[6144,1024]{1,0:T(8,128)(2,1)} %all-gather.2.cloned.1.call-done, s32[4096]{0:T(1024)S(1)} %fusion.38), kind=kCustom, calls=%fused_computation.1 | custom fusion | bytes 16793600 | tf_op jit(solution)/shard_map/jit(_take)/gather | solution.py:21
  193.8 0.0 copy-start.3
  193.8 9.6 %multiply_convert_fusion = bf16[512,1024]{1,0:T(8,128)(2,1)S(1)} fusion(bf16[512,1024]{1,0:T(8,128)(2,1)S(1)} %fusion.28, bf16[4096,1024]{1,0:T(8,128)(2,1)} %gather_fusion.1, pred[4096]{0:T(1024)(128)(4,1)S(1)} %get-tuple-element.6, bf16[512,4096]{1,0:T(8,128)(2,1)} %param.6, f32[4096]{0:T(1024)S(1)} %get-tuple-element.5, f32[512]{0:T(512)S(1)} %add_rsqrt_fusion, ...), kind=kOutput, calls=%fused_computation.28 | convolution fusion | flops 4313841664 | bytes 14704640 | tf_op jit(solution)/shard_map/dot_general | solution.py:61
  203.4 0.0 copy-done.3
  203.4 7.9 %convolution_convert_fusion = bf16[4096,1024]{1,0:T(8,128)(2,1)} fusion(bf16[512,1024]{1,0:T(8,128)(2,1)S(1)} %multiply_convert_fusion, bf16[512,4096]{1,0:T(8,128)(2,1)S(1)} %copy-done.3, f32[4096]{0:T(1024)S(1)} %get-tuple-element.5, f32[512]{0:T(512)S(1)} %add_rsqrt_fusion, f32[512]{0:T(512)S(1)} %broadcast_multiply_fusion), kind=kOutput, calls=%fused_computation.20 | convolution fusion | flops 4309647360 | bytes 13651968 | tf_op jit(solution)/shard_map/dot_general | solution.py:67
  211.3 0.0 reduce-scatter.2.cloned.1.call-update
  211.4 84.6 %reduce-scatter.2.cloned.1.call-done = bf16[256,1024]{1,0:T(8,128)(2,1)} async-done(((bf16[4096,1024]{1,0:T(8,128)(2,1)}), bf16[256,1024]{1,0:T(8,128)(2,1)}) %reduce-scatter.2.cloned.1.call-update) | async-done | bytes 524304 | tf_op jit(solution)/shard_map/reduce_scatter | solution.py:66
  296.0 2.1 convert_element_type.62
  (15 shorter events, 0.2 us)
Async XLA Ops:
  6.5 71.3 %copy-start = (bf16[512,1536]{1,0:T(8,128)(2,1)S(1)}, bf16[512,1536]{1,0:T(8,128)(2,1)}, u32[]{:S(2)}) copy-start(bf16[512,1536]{1,0:T(8,128)(2,1)} %param.7) | copy-start | bytes 4718596
  49.0 26.1 %all-to-all-start = ((bf16[384,8,256]{0,2,1:T(8,128)(2,1)}), bf16[384,8,256]{0,2,1:T(8,128)(2,1)S(1)}, u32[]{:S(2)}, u32[]{:S(2)}) async-start(bf16[384,8,256]{0,2,1:T(8,128)(2,1)} %bitcast.47), calls=%async_computation | async-start | bytes 3145728 | tf_op jit(solution)/shard_map/all_to_all | solution.py:55
  53.5 113.3 %all-gather.2.cloned.1.call-start = ((), (), s32[]{:S(2)}) async-start(), calls=%async_computation.3 | async-start | bytes 13369344 | tf_op jit(solution)/shard_map/all_gather | solution.py:20
  82.6 4.7 %copy-start.4 = (s32[4096]{0:T(1024)S(1)}, s32[4096]{0:T(1024)}, u32[]{:S(2)}) copy-start(s32[4096]{0:T(1024)} %param.10) | copy-start | bytes 49156
  82.6 4.8 %copy-start.1 = (f32[6144]{0:T(1024)S(1)}, f32[6144]{0:T(1024)}, u32[]{:S(2)}) copy-start(f32[6144]{0:T(1024)} %param.9) | copy-start | bytes 73732
  82.6 32.5 %all-to-all-start.1 = ((bf16[512,8,256]{0,2,1:T(8,128)(2,1)}), bf16[512,8,256]{0,2,1:T(8,128)(2,1)}, u32[]{:S(2)}, u32[]{:S(2)}) async-start(bf16[512,8,256]{0,2,1:T(8,128)(2,1)} %bitcast.45), calls=%async_computation.1 | async-start | bytes 4194304 | tf_op jit(solution)/shard_map/all_to_all | solution.py:56
  87.1 208.9 %reduce-scatter.2.cloned.1.call-start = ((), (), s32[]{:S(2)}) async-start(), calls=%async_computation.4 | async-start | bytes 8912896 | tf_op jit(solution)/shard_map/reduce_scatter | solution.py:66
  110.4 3.5 %copy-start.2 = (bf16[512,4096]{1,0:T(8,128)(2,1)S(1)}, bf16[512,4096]{1,0:T(8,128)(2,1)}, u32[]{:S(2)}) copy-start(bf16[512,4096]{1,0:T(8,128)(2,1)} %param.6) | copy-start | bytes 12582916
  193.8 9.6 %copy-start.3 = (bf16[512,4096]{1,0:T(8,128)(2,1)S(1)}, bf16[512,4096]{1,0:T(8,128)(2,1)}, u32[]{:S(2)}) copy-start(bf16[512,4096]{1,0:T(8,128)(2,1)} %param.6) | copy-start | bytes 12582916
Sparse Core Ops, SparseCore 0:
  78.0 88.7 all-gather.1
  211.5 84.4 reduce-scatter.1
where the time goes:
time: 308 us; the launch traced here: 305 us
  waiting for transfers between devices  149 us (48%)
  local copies, waits for them, and re-layouts  81.7 us (27%)
  matrix products  34.9 us (11%)
  other arithmetic  16.7 us (5%)
  between operations  13.6 us (4%)
  starting transfers between devices  9.21 us (3%)
    reduce_scatter x1, waiting for transfers between devices, per_device(): lax.psum_scatter(lax.dot_general(normed, delta, (((0,), (0,)), ((), ())),...  84.6 us
    all_gather x1, waiting for transfers between devices, kept_matrix(): gathered = lax.all_gather(weight_cols, 'dp', axis=0, tiled=True)  47.6 us
    unnamed x11, local copies, waits for them, and re-layouts  30.9 us
    gather x1, local copies, waits for them, and re-layouts, kept_matrix(): return jnp.take(gathered, keep_chan, axis=0)  27.1 us
    gather x1, local copies, waits for them, and re-layouts, per_device(): gain = jnp.take(gain_old, keep_chan)  23 us
    dot_general x4, matrix products, pick_columns(): jnp.dot(matrix, table, preferred_element_type=jnp.float32)  17.4 us
    all_to_all x1, waiting for transfers between devices, per_device(): lax.all_to_all(packed_weight, 'tensor', split_axis=1, concat_axis=1, tile...  16.6 us
    dot_general x1, matrix products, per_device(): jnp.dot(normed, kept_matrix(weight_cols, keep_chan), preferred_element_ty...  9.6 us
  transfers between devices with their start and end apart: 4, of which 3 were waited for; matrix products, arithmetic and copies ran while one was open for 13% of the time, Pallas kernels for 0%

commit v1 on v0

v1 whole, which is shorter than its diff:
```python
import math

import jax
import jax.numpy as jnp
from jax import lax
from jax.experimental import pallas as pl
from jax.experimental.pallas import tpu as pltpu
from jax.sharding import PartitionSpec as P

MESH = pl.DeviceIdType.MESH
SLOT_ROWS = 320
SLOT_COLS = 256
BF16 = jnp.bfloat16
F32 = jnp.float32


def ranks_of(hits):
    rows, width = hits.shape
    chunks = width // 128
    parts = hits.astype(BF16).reshape(rows * chunks, 128)
    before = (jnp.arange(128)[:, None] < jnp.arange(128)[None, :]).astype(BF16)
    within = jnp.dot(parts, before, preferred_element_type=F32).reshape(rows, chunks, 128)
    totals = jnp.sum(hits.astype(F32).reshape(rows, chunks, 128), axis=2).astype(BF16)
    ahead = (jnp.arange(chunks)[:, None] < jnp.arange(chunks)[None, :]).astype(BF16)
    starts = jnp.dot(totals, ahead, preferred_element_type=F32)
    return (within + starts[:, :, None]).reshape(rows, width).astype(jnp.int32)


def kernel(
    scale,
    tokens_hbm, teacher_hbm, up_ref, gain_ref, cols_ref, rowsel_ref, from_ref, pos_hbm,
    out_ref,
    normed, normed_t, packed_x, weights, teacher, kept_rows, weight_send, weight_recv,
    target_send, target_recv, unpack, places, pick, pre, delta, target, ring_b, ring_a,
    local_sems, ws_send, ws_recv, ts_send, ts_recv, ag_send, ag_recv, rs_send, rs_recv,
):
    dp = lax.axis_index("dp")
    owner = lax.axis_index("tensor")
    core = owner % 2
    z, x = dp // 4, dp % 4
    a = x + core * (z - x)
    b = z + core * (x - z)

    def dp_of(ao, bo):
        aa, bb = (a + ao) % 4, (b + bo) % 4
        return bb * 4 + aa + core * 3 * (aa - bb)

    def device(ao, bo):
        return (dp_of(ao, bo), owner)

    load_tokens = pltpu.make_async_copy(tokens_hbm, packed_x.at[:, pl.ds(0, 4096)], local_sems.at[0])
    load_teacher = pltpu.make_async_copy(teacher_hbm, teacher, local_sems.at[1])
    load_places = pltpu.make_async_copy(pos_hbm, places, local_sems.at[2])
    load_teacher.start()
    load_tokens.start()
    load_places.start()
    barrier = pltpu.get_barrier_semaphore()
    for ao, bo in ((1, 0), (3, 0), (0, 1), (0, 3)):
        pl.semaphore_signal(barrier, inc=1, device_id=device(ao, bo), device_id_type=MESH)
    for k in range(1, 8):
        pl.semaphore_signal(barrier, inc=1, device_id=(dp, (owner + k) % 8), device_id_type=MESH)

    rows_hot = (lax.broadcasted_iota(jnp.int32, (SLOT_ROWS, 384), 1) == rowsel_ref[...]).astype(F32).astype(BF16)
    kept_rows[...] = jnp.dot(rows_hot, up_ref[...], preferred_element_type=F32).astype(BF16)
    load_teacher.wait()

    def pack(o, carry):
        hot = (
            lax.broadcasted_iota(jnp.int32, (1536, SLOT_COLS), 0) == cols_ref[pl.ds(o, 1), :]
        ).astype(F32).astype(BF16)
        pick[pl.ds(0, 1536), :] = hot
        weight_send[o] = jnp.dot(kept_rows[...], pick[pl.ds(0, 1536), :], preferred_element_type=F32).astype(BF16)
        target_send[o] = jnp.dot(teacher[...], pick[pl.ds(0, 1536), :], preferred_element_type=F32).astype(BF16)
        return carry

    lax.fori_loop(0, 8, pack, 0)
    pl.semaphore_wait(barrier, 11)

    def weight_copy(k, h):
        peer = (owner + k) % 8
        return pltpu.make_async_remote_copy(
            src_ref=weight_send.at[peer, pl.ds(h * 160, 160), :],
            dst_ref=weight_recv.at[owner, pl.ds(h * 160, 160), :],
            send_sem=ws_send.at[h * 8 + k],
            recv_sem=ws_recv.at[h * 8 + k],
            device_id=(dp, peer),
            device_id_type=MESH,
        )

    def target_copy(k):
        peer = (owner + k) % 8
        return pltpu.make_async_remote_copy(
            src_ref=target_send.at[peer],
            dst_ref=target_recv.at[owner],
            send_sem=ts_send.at[k],
            recv_sem=ts_recv.at[k],
            device_id=(dp, peer),
            device_id_type=MESH,
        )

    for h in range(2):
        for k in (4, 3, 5, 2, 6, 1, 7):
            weight_copy(k, h).start()
    weight_recv[owner] = weight_send[owner]
    target_recv[owner] = target_send[owner]

    def make_unpack(s, carry):
        unpack[pl.ds(pl.multiple_of(s * 256, 256), 256), :] = (
            lax.broadcasted_iota(jnp.int32, (256, 1024), 0) + s * 256 == from_ref[...]
        ).astype(F32).astype(BF16)
        return carry

    lax.fori_loop(0, 8, make_unpack, 0)
    load_tokens.wait()

    def norm(r, carry):
        rows = pl.ds(pl.multiple_of(r * 16, 16), 16)
        values = packed_x[rows, pl.ds(0, 4096)].astype(F32)
        center = jnp.mean(values, axis=1, keepdims=True)
        spread = jnp.mean((values - center) ** 2, axis=1, keepdims=True)
        normed[rows, :] = ((values - center) * lax.rsqrt(spread + 1e-05) * gain_ref[...]).astype(BF16)
        return carry

    def slot_row(ao, bo, h):
        aa, bb = (a + ao) % 4, (b + bo) % 4
        return pl.multiple_of((bb * 4 + aa) * SLOT_ROWS + h * 160, 32)

    ag_started = []

    def ag_copy(ring, step, ao, bo, h):
        far = (ao if ring == 0 else bo) != 0
        role = (4 + h) if far else ((0 if step == 1 else 2) + h)
        index = role if ring == 0 else 6 + ao * 6 + role
        rows = pl.ds(slot_row(ao, bo, h), 160)
        return pltpu.make_async_remote_copy(
            src_ref=weights.at[rows, :],
            dst_ref=weights.at[rows, :],
            send_sem=ag_send.at[len(ag_started)],
            recv_sem=ag_recv.at[index],
            device_id=device(step, 0) if ring == 0 else device(0, step),
            device_id_type=MESH,
        )

    def ag_start(ring, step, ao, bo, h):
        copy = ag_copy(ring, step, ao, bo, h)
        copy.start()
        ag_started.append(copy)

    def ag_wait(ring, ao, bo, h):
        offset = ao if ring == 0 else bo
        role = {3: 0, 1: 2, 2: 4}[offset] + h
        index = role if ring == 0 else 6 + ao * 6 + role
        rows = pl.ds(slot_row(ao, bo, h), 160)
        pltpu.make_async_remote_copy(
            src_ref=weights.at[rows, :],
            dst_ref=weights.at[rows, :],
            send_sem=ag_send.at[0],
            recv_sem=ag_recv.at[index],
            device_id=device(1, 0),
            device_id_type=MESH,
        ).wait_recv()

    lax.fori_loop(0, 16, norm, 0)
    for h in range(2):
        for k in range(1, 8):
            source = (owner - k + 8) % 8
            pltpu.make_async_remote_copy(
                src_ref=weight_recv.at[source, pl.ds(h * 160, 160), :],
                dst_ref=weight_recv.at[source, pl.ds(h * 160, 160), :],
                send_sem=ws_send.at[h * 8 + k],
                recv_sem=ws_recv.at[h * 8 + k],
                device_id=(dp, (owner + k) % 8),
                device_id_type=MESH,
            ).wait_recv()
        total = jnp.zeros((160, 1024), F32)
        for s in range(8):
            total += jnp.dot(
                weight_recv[s, h * 160 : h * 160 + 160, :],
                unpack[s * 256 : s * 256 + 256, :],
                preferred_element_type=F32,
            )
        weights[pl.ds(slot_row(0, 0, h), 160), :] = total.astype(BF16)
        for ring in (0, 1):
            for step in (1, 3):
                ag_start(ring, step, 0, 0, h)
    for k in (4, 3, 5, 2, 6, 1, 7):
        target_copy(k).start()
    lax.fori_loop(16, 32, norm, 0)

    def permute(c, carry):
        start = pl.multiple_of(c * 256, 256)
        lanes = lax.broadcasted_iota(jnp.int32, (4096, 128), 1) + start
        pick[:, pl.ds(0, 128)] = (places[...] == lanes).astype(F32).astype(BF16)
        pick[:, pl.ds(128, 128)] = (places[...] == lanes + 128).astype(F32).astype(BF16)
        packed_x[:, pl.ds(start, 256)] = jnp.dot(normed[...], pick[...], preferred_element_type=F32).astype(BF16)
        return carry

    def permute_group(bo):
        first = ((b + bo) % 4) * 5
        lax.fori_loop(first, first + 5, permute, 0)

    def transpose(ao, bo):
        aa, bb = (a + ao) % 4, (b + bo) % 4
        cols = pl.ds(pl.multiple_of(dp_of(ao, bo) * 256, 256), 256)
        rows = pl.ds(pl.multiple_of((aa * 4 + bb) * 256, 256), 256)
        normed_t[rows, :] = normed[:, cols].T

    def multiply_group(bo, first):
        depth = pl.ds(pl.multiple_of(((b + bo) % 4) * 1280, 256), 1280)

        @pl.loop(0, 4)
        def _(n):
            cols = pl.ds(pl.multiple_of(n * 256, 256), 256)
            part = jnp.dot(packed_x[:, depth], weights[depth, cols], preferred_element_type=F32)
            pre[:, cols] = part if first else pre[:, cols] + part

    load_places.wait()

    for ao, h in ((3, 0), (1, 1), (3, 1), (1, 0)):
        ag_wait(0, ao, 0, h)
        if (ao, h) == (3, 0):
            ag_start(0, 1, 3, 0, 0)
        if (ao, h) == (1, 1):
            ag_start(0, 3, 1, 0, 1)
        ag_start(1, 1, ao, 0, h)
        ag_start(1, 3, ao, 0, h)
    ag_wait(1, 0, 3, 0)
    ag_start(1, 1, 0, 3, 0)
    ag_wait(1, 0, 1, 1)
    ag_start(1, 3, 0, 1, 1)
    for h in range(2):
        ag_wait(0, 2, 0, h)
        ag_start(1, 1, 2, 0, h)
        ag_start(1, 3, 2, 0, h)
    permute_group(0)
    for ao in (3, 1):
        ag_wait(1, ao, 3, 0)
        ag_start(1, 1, ao, 3, 0)
        ag_wait(1, ao, 1, 1)
        ag_start(1, 3, ao, 1, 1)
    permute_group(3)
    ag_wait(1, 2, 3, 0)
    ag_start(1, 1, 2, 3, 0)
    ag_wait(1, 2, 1, 1)
    ag_start(1, 3, 2, 1, 1)
    multiply_group(0, True)
    permute_group(1)
    permute_group(2)

    @pl.loop(0, 16)
    def _(s):
        aa, bb = s // 4, s % 4
        cols = pl.ds(pl.multiple_of((bb * 4 + aa + core * 3 * (aa - bb)) * 256, 256), 256)
        normed_t[pl.ds(pl.multiple_of(s * 256, 256), 256), :] = normed[:, cols].T

    for k in range(1, 8):
        source = (owner - k + 8) % 8
        pltpu.make_async_remote_copy(
            src_ref=target_recv.at[source],
            dst_ref=target_recv.at[source],
            send_sem=ts_send.at[k],
            recv_sem=ts_recv.at[k],
            device_id=(dp, (owner + k) % 8),
            device_id_type=MESH,
        ).wait_recv()

    @pl.loop(0, 4)
    def _(n):
        cols = pl.ds(pl.multiple_of(n * 256, 256), 256)
        total = jnp.zeros((512, 256), F32)
        for s in range(8):
            total += jnp.dot(target_recv[s], unpack[s * 256 : s * 256 + 256, cols], preferred_element_type=F32)
        target[:, cols] = total.astype(BF16)

    for ao in range(4):
        ag_wait(1, ao, 3, 1)
        ag_wait(1, ao, 1, 0)
    multiply_group(3, False)
    multiply_group(1, False)
    for ao in range(4):
        ag_wait(1, ao, 2, 0)
        ag_wait(1, ao, 2, 1)
    multiply_group(2, False)

    @pl.loop(0, 32)
    def _(r):
        rows = pl.ds(pl.multiple_of(r * 16, 16), 16)
        active = jnp.maximum(pre[rows, :], 0.0)
        delta[rows, :] = (2.0 * active * (active * active - target[rows, :].astype(F32)) * scale).astype(BF16)

    for copy in ag_started:
        copy.wait_send()
    for k in range(1, 8):
        for h in range(2):
            weight_copy(k, h).wait_send()
        target_copy(k).wait_send()

    rs_started = []

    def grad_row(ao, bo, h):
        aa, bb = (a + ao) % 4, (b + bo) % 4
        return pl.multiple_of((aa * 4 + bb) * 256 + h * 128, 128)

    def rs_start(ring, step, ao, bo, h, role):
        index = role if ring == 0 else 6 + ao * 6 + role
        place = ring_a.at[pl.ds(role * 128, 128), :] if ring == 0 else ring_b.at[pl.ds((ao * 6 + role) * 128, 128), :]
        copy = pltpu.make_async_remote_copy(
            src_ref=weights.at[pl.ds(grad_row(ao, bo, h), 128), :],
            dst_ref=place,
            send_sem=rs_send.at[len(rs_started)],
            recv_sem=rs_recv.at[index],
            device_id=device(step, 0) if ring == 0 else device(0, step),
            device_id_type=MESH,
        )
        copy.start()
        rs_started.append(copy)

    def rs_take(ring, ao, role):
        index = role if ring == 0 else 6 + ao * 6 + role
        place = ring_a.at[pl.ds(role * 128, 128), :] if ring == 0 else ring_b.at[pl.ds((ao * 6 + role) * 128, 128), :]
        pltpu.make_async_remote_copy(
            src_ref=place,
            dst_ref=place,
            send_sem=rs_send.at[0],
            recv_sem=rs_recv.at[index],
            device_id=device(1, 0),
            device_id_type=MESH,
        ).wait_recv()
        return place

    def add_into(ao, bo, h, places_in, final=False):
        base = grad_row(ao, bo, h)

        @pl.loop(0, 8)
        def _(r):
            total = weights[pl.ds(base + r * 16, 16), :].astype(F32)
            for place in places_in:
                total += place[pl.ds(pl.multiple_of(r * 16, 16), 16), :].astype(F32)
            if final:
                out_ref[pl.ds(pl.multiple_of(h * 128 + r * 16, 16), 16), :] = total
            else:
                weights[pl.ds(base + r * 16, 16), :] = total.astype(BF16)

    def products(ao):
        rows = pl.ds(pl.multiple_of(((a + ao) % 4) * 1024, 1024), 1024)

        @pl.loop(0, 4)
        def _(n):
            cols = pl.ds(pl.multiple_of(n * 256, 256), 256)
            weights[rows, cols] = jnp.dot(
                normed_t[rows, :], delta[:, cols], preferred_element_type=F32
            ).astype(BF16)

    def spread_b(ao):
        rs_start(1, 1, ao, 2, 0, 0)
        rs_start(1, 3, ao, 2, 1, 1)
        rs_start(1, 1, ao, 1, 1, 3)
        rs_start(1, 3, ao, 3, 0, 4)

    def relay_b(ao):
        add_into(ao, 1, 0, [rs_take(1, ao, 0)])
        rs_start(1, 1, ao, 1, 0, 2)
        add_into(ao, 3, 1, [rs_take(1, ao, 1)])
        rs_start(1, 3, ao, 3, 1, 5)

    def gather_b(ao):
        for h in range(2):
            add_into(ao, 0, h, [rs_take(1, ao, 2 + h), rs_take(1, ao, 4 + h)])

    products(2)
    spread_b(2)
    products(1)
    spread_b(1)
    relay_b(2)
    products(3)
    spread_b(3)
    relay_b(1)
    products(0)
    spread_b(0)
    relay_b(3)
    gather_b(2)
    rs_start(0, 1, 2, 0, 0, 0)
    rs_start(0, 3, 2, 0, 1, 1)
    relay_b(0)
    gather_b(1)
    rs_start(0, 1, 1, 0, 1, 3)
    add_into(1, 0, 0, [rs_take(0, 0, 0)])
    rs_start(0, 1, 1, 0, 0, 2)
    gather_b(3)
    rs_start(0, 3, 3, 0, 0, 4)
    add_into(3, 0, 1, [rs_take(0, 0, 1)])
    rs_start(0, 3, 3, 0, 1, 5)
    for h in range(2):
        add_into(
            0, 0, h,
            [rs_take(1, 0, 2 + h), rs_take(1, 0, 4 + h), rs_take(0, 0, 2 + h), rs_take(0, 0, 4 + h)],
            final=True,
        )
    for copy in rs_started:
        copy.wait_send()


def per_device(tokens_in, teacher_hidden, up_old, gain_old, keep_chan, keep_ff):
    dp = lax.axis_index("dp")
    owner = lax.axis_index("tensor")
    core = owner % 2
    scale = 1.0 / math.sqrt(tokens_in.shape[0] * lax.axis_size("dp"))

    blocks = keep_ff.reshape(8, 1024)
    local = blocks - owner * 1536
    mine = (local >= 0) & (local < 1536)
    slot = jnp.where(mine, ranks_of(mine), -1)
    cols = jnp.sum(
        jnp.where(slot[:, None, :] == jnp.arange(SLOT_COLS)[None, :, None], local[:, None, :] + 1, 0), axis=2
    ) - 1

    own = lax.dynamic_slice_in_dim(keep_ff, owner * 1024, 1024)
    source_hits = own[None, :] // 1536 == jnp.arange(8)[:, None]
    where_from = jnp.sum(
        jnp.where(source_hits, ranks_of(source_hits) + jnp.arange(8)[:, None] * SLOT_COLS, 0), axis=0
    )

    block = keep_chan // 384
    block_hits = block[None, :] == jnp.arange(16)[:, None]
    rank = jnp.sum(jnp.where(block_hits, ranks_of(block_hits), 0), axis=0)
    turned = (block % 4) * 4 + block // 4
    order = jnp.where(core == 0, block, turned)
    pos = order * SLOT_ROWS + rank
    pos = jnp.broadcast_to(pos[:, None], (4096, 128))
    rank_here = jnp.where(block == dp, rank, -1)
    rowsel = jnp.sum(
        jnp.where(rank_here[None, :] == jnp.arange(SLOT_ROWS)[:, None], keep_chan[None, :] - dp * 384 + 1, 0),
        axis=1, keepdims=True,
    ) - 1

    high = (keep_chan[None, :] // 128 == jnp.arange(48)[:, None]).astype(F32)
    low = keep_chan[None, :] % 128 == jnp.arange(128)[:, None]
    wide = lax.dot_general(
        gain_old.reshape(48, 128), high, (((0,), (0,)), ((), ())),
        precision=lax.Precision.HIGHEST, preferred_element_type=F32,
    )
    gain = jnp.sum(jnp.where(low, wide, 0.0), axis=0, keepdims=True)

    anywhere = pl.BlockSpec(memory_space=pl.ANY)
    vmem = pl.BlockSpec(memory_space=pltpu.VMEM)
    dma = pltpu.SemaphoreType.DMA

    def body(*refs):
        kernel(scale, *refs)

    return pl.pallas_call(
        body,
        out_shape=jax.ShapeDtypeStruct((256, 1024), F32),
        in_specs=[anywhere, anywhere, vmem, vmem, vmem, vmem, vmem, anywhere],
        out_specs=vmem,
        scratch_shapes=[
            pltpu.VMEM((512, 4096), BF16),
            pltpu.VMEM((4096, 512), BF16),
            pltpu.VMEM((512, 5120), BF16),
            pltpu.VMEM((5120, 1024), BF16),
            pltpu.VMEM((512, 1536), BF16),
            pltpu.VMEM((SLOT_ROWS, 1536), BF16),
            pltpu.VMEM((8, SLOT_ROWS, SLOT_COLS), BF16),
            pltpu.VMEM((8, SLOT_ROWS, SLOT_COLS), BF16),
            pltpu.VMEM((8, 512, SLOT_COLS), BF16),
            pltpu.VMEM((8, 512, SLOT_COLS), BF16),
            pltpu.VMEM((2048, 1024), BF16),
            pltpu.VMEM((4096, 128), jnp.int32),
            pltpu.VMEM((4096, 256), BF16),
            pltpu.VMEM((512, 1024), F32),
            pltpu.VMEM((512, 1024), BF16),
            pltpu.VMEM((512, 1024), BF16),
            pltpu.VMEM((24 * 128, 1024), BF16),
            pltpu.VMEM((6 * 128, 1024), BF16),
            dma((3,)),
            dma((16,)),
            dma((16,)),
            dma((8,)),
            dma((8,)),
            dma((30,)),
            dma((30,)),
            dma((30,)),
            dma((30,)),
        ],
        compiler_params=pltpu.CompilerParams(
            collective_id=0, has_side_effects=True, vmem_limit_bytes=62 * 1024 * 1024
        ),
        cost_estimate=pl.CostEstimate(flops=40_000_000_000, bytes_accessed=10_000_000, transcendentals=0),
    )(tokens_in, teacher_hidden, up_old, gain, cols, rowsel, where_from[None, :], pos)


def solution(mesh):
    return jax.shard_map(
        per_device,
        mesh=mesh,
        in_specs=(P("dp", None), P("dp", "tensor"), P("dp", "tensor"), P(), P(), P()),
        out_specs=P("dp", "tensor"),
        check_vma=False,
    )
```

time: 308 us -> 164 us (0.53)
  waiting for transfers between devices: 149 us -> 0 us
  Pallas kernels: 0 us -> 148 us
  local copies, waits for them, and re-layouts: 81.7 us -> 6.04 us
  matrix products: 34.9 us -> 3.2 us
  between operations: 13.6 us -> 0.05 us
  other arithmetic: 16.7 us -> 6.48 us
  starting transfers between devices: 9.21 us -> 0 us
    pallas_call x0 -> x1, Pallas kernels: none -> 148 us  [per_device(): pl.pallas_call(body, out_shape=jax.ShapeDtypeStruct((256, 1024), F32), in...]
    reduce_scatter x1 -> x0, waiting for transfers between devices: 84.6 us -> none  [per_device(): lax.psum_scatter(lax.dot_general(normed, delta, (((0,), (0,)), ((), ())),...]
    gather x2 -> x0, local copies, waits for them, and re-layouts: 50.1 us -> none  [the longest x1 27.1 us: kept_matrix(): return jnp.take(gathered, keep_chan, axis=0)]
    all_gather x1 -> x0, waiting for transfers between devices: 47.6 us -> none  [kept_matrix(): gathered = lax.all_gather(weight_cols, 'dp', axis=0, tiled=True)]
    dot_general x6 -> x7, matrix products: 34.9 us -> 3.2 us  [the longest x1 1.78 us: per_device(): lax.dot_general(gain_old.reshape(48, 128), high, (((0,), (0,)), ((), ()))...]
    unnamed x11 -> x3, local copies, waits for them, and re-layouts: 30.9 us -> 2.31 us
    all_to_all x2 -> x0, waiting for transfers between devices: 16.6 us -> none  [the longest x1 16.6 us: per_device(): lax.all_to_all(packed_weight, 'tensor', split_axis=1, concat_axis=1, tile...]
    all_to_all x2 -> x0, starting transfers between devices: 8.95 us -> none  [the longest x1 4.48 us: per_device(): lax.all_to_all(packed_target, 'tensor', split_axis=1, concat_axis=1, tile...]
  transfers between devices with their start and end apart: 4 -> 0, of which waited for: 3 -> 0; matrix products, arithmetic and copies ran while one was open for 13% -> 0% of each run, Pallas kernels for 0% -> 0%
where the time goes in v1:
time: 164 us
  Pallas kernels  148 us (90%)
  other arithmetic  6.48 us (4%)
  local copies, waits for them, and re-layouts  6.04 us (4%)
  matrix products  3.2 us (2%)
    pallas_call x1, Pallas kernels, per_device(): pl.pallas_call(body, out_shape=jax.ShapeDtypeStruct((256, 1024), F32), in...  148 us

profile of v1, /device:TPU:34, one launch (start us, length us, event | category | flops | bytes accessed | tf_op | source)
XLA Modules:
  0.0 163.7 jit_solution(18008210279134441387)
XLA Ops:
  0.0 0.0 copy-start
  0.0 0.7 fusion.31
  0.7 0.1 convert_reduce_fusion.1
  0.8 0.1 fusion.33
  0.9 0.7 fusion.10
  1.7 0.9 convert_reduce_fusion.2
  2.5 0.1 fusion.34
  2.7 0.7 fusion.38
  3.4 0.1 convert_reduce_fusion
  3.6 0.1 fusion.28
  3.7 0.2 fusion.4
  3.9 0.1 fusion.9
  4.0 0.1 bitcast_select_fusion
  4.1 0.8 subtract_add_fusion
  4.8 1.0 select_reduce_fusion
  5.8 0.6 broadcast_add_fusion.refs_4_
  6.4 0.8 fusion.23
  7.2 0.8 select_reduce_fusion.1
  8.0 0.0 copy-done
  8.0 1.8 %fusion.1 = f32[4096]{0:T(1024)} fusion(s32[4096]{0:T(1024)S(1)} %get-tuple-element.9, s32[4096]{0:T(1024)S(1)} %get-tuple-element.10, f32[6144]{0:T(1024)S(1)} %copy-done), kind=kOutput, calls=%fused_computation.7 | convolution fusion | flops 303755264 | bytes 73728 | tf_op jit(solution)/shard_map/dot_general | solution.py:438
  9.8 0.8 sub.68.refs_5_
  10.5 2.9 %broadcast_in_dim.53.refs_7_ = s32[4096,128]{1,0:T(8,128)} broadcast(s32[4096]{0:T(1024)S(1)} %get-tuple-element.7), dimensions={0} | broadcast | bytes 2113536 | tf_op jit(solution)/shard_map/broadcast_in_dim | solution.py:429
  13.5 147.9 %shard_map.64 = f32[256,1024]{1,0:T(8,128)} custom-call(bf16[512,4096]{1,0:T(8,128)(2,1)} %refs_0_.1, bf16[512,1536]{1,0:T(8,128)(2,1)} %refs_1_.1, bf16[384,1536]{1,0:T(8,128)(2,1)} %refs_2_.1, f32[1,4096]{1,0:T(1,128)} %bitcast.34, s32[8,256]{1,0:T(8,128)} %broadcast_add_fusion.refs_4_, s32[320,1]{1,0:T(8,128)} %sub.68.refs_5_, s32[1,1024]{1,0:T(1,128)} %bitcast.35, ...), custom_call_target="tpu_custom_call" | custom-call | flops 40000000000 | bytes 10000000 | tf_op jit(solution)/shard_map/pallas_call | solution.py:451
  161.4 2.3 %copy.12 = f32[256,1024]{1,0:T(8,128)} copy(f32[256,1024]{1,0:T(8,128)} %shard_map.64) | data formatting | bytes 2097152
  (4 shorter events, 0.0 us)
Async XLA Ops:
  0.0 8.0 %copy-start = (f32[6144]{0:T(1024)S(1)}, f32[6144]{0:T(1024)}, u32[]{:S(2)}) copy-start(f32[6144]{0:T(1024)} %param.9) | copy-start | bytes 73732

commit v2 on v1

--- a/solution.py
+++ b/solution.py
@@ -14,24 +14,34 @@
 F32 = jnp.float32
 
 
-def ranks_of(hits):
-    rows, width = hits.shape
-    chunks = width // 128
-    parts = hits.astype(BF16).reshape(rows * chunks, 128)
-    before = (jnp.arange(128)[:, None] < jnp.arange(128)[None, :]).astype(BF16)
-    within = jnp.dot(parts, before, preferred_element_type=F32).reshape(rows, chunks, 128)
-    totals = jnp.sum(hits.astype(F32).reshape(rows, chunks, 128), axis=2).astype(BF16)
-    ahead = (jnp.arange(chunks)[:, None] < jnp.arange(chunks)[None, :]).astype(BF16)
-    starts = jnp.dot(totals, ahead, preferred_element_type=F32)
-    return (within + starts[:, :, None]).reshape(rows, width).astype(jnp.int32)
+def strict(shape, dim, group):
+    rows = lax.broadcasted_iota(jnp.int32, shape, 0)
+    cols = lax.broadcasted_iota(jnp.int32, shape, 1)
+    ahead = rows < cols if dim == 1 else cols < rows
+    same = rows // group == cols // group
+    return jnp.where(ahead & same, 1.0, 0.0).astype(BF16)
+
+
+def ranks_of(hits, group):
+    parts = hits.astype(BF16)
+    within = jnp.dot(parts, strict((128, 128), 1, 128), preferred_element_type=F32)
+    above = jnp.dot(strict((hits.shape[0],) * 2, 0, group), parts, preferred_element_type=F32)
+    return within + jnp.sum(above, axis=1, keepdims=True)
+
+
+def blocks_of(index, width, count):
+    block = jnp.zeros_like(index)
+    for edge in range(1, count):
+        block += jnp.where(index >= edge * width, 1, 0)
+    return block
 
 
 def kernel(
     scale,
-    tokens_hbm, teacher_hbm, up_ref, gain_ref, cols_ref, rowsel_ref, from_ref, pos_hbm,
+    tokens_hbm, teacher_hbm, up_hbm, gain_ref, chan_ref, ff_ref,
     out_ref,
-    normed, normed_t, packed_x, weights, teacher, kept_rows, weight_send, weight_recv,
-    target_send, target_recv, unpack, places, pick, pre, delta, target, ring_b, ring_a,
+    normed, normed_t, packed_x, weights, teacher, up, kept_rows, weight_send, weight_recv,
+    target_send, target_recv, unpack, picks, pre, delta, target, ring_b, ring_a, gain, places,
     local_sems, ws_send, ws_recv, ts_send, ts_recv, ag_send, ag_recv, rs_send, rs_recv,
 ):
     dp = lax.axis_index("dp")
@@ -48,33 +58,65 @@
     def device(ao, bo):
         return (dp_of(ao, bo), owner)
 
-    load_tokens = pltpu.make_async_copy(tokens_hbm, packed_x.at[:, pl.ds(0, 4096)], local_sems.at[0])
+    load_up = pltpu.make_async_copy(up_hbm, up, local_sems.at[0])
     load_teacher = pltpu.make_async_copy(teacher_hbm, teacher, local_sems.at[1])
-    load_places = pltpu.make_async_copy(pos_hbm, places, local_sems.at[2])
+    load_tokens = pltpu.make_async_copy(tokens_hbm, packed_x.at[:, pl.ds(0, 4096)], local_sems.at[2])
+    load_up.start()
     load_teacher.start()
     load_tokens.start()
-    load_places.start()
     barrier = pltpu.get_barrier_semaphore()
     for ao, bo in ((1, 0), (3, 0), (0, 1), (0, 3)):
         pl.semaphore_signal(barrier, inc=1, device_id=device(ao, bo), device_id_type=MESH)
     for k in range(1, 8):
         pl.semaphore_signal(barrier, inc=1, device_id=(dp, (owner + k) % 8), device_id_type=MESH)
 
-    rows_hot = (lax.broadcasted_iota(jnp.int32, (SLOT_ROWS, 384), 1) == rowsel_ref[...]).astype(F32).astype(BF16)
-    kept_rows[...] = jnp.dot(rows_hot, up_ref[...], preferred_element_type=F32).astype(BF16)
-    load_teacher.wait()
-
-    def pack(o, carry):
-        hot = (
-            lax.broadcasted_iota(jnp.int32, (1536, SLOT_COLS), 0) == cols_ref[pl.ds(o, 1), :]
-        ).astype(F32).astype(BF16)
-        pick[pl.ds(0, 1536), :] = hot
-        weight_send[o] = jnp.dot(kept_rows[...], pick[pl.ds(0, 1536), :], preferred_element_type=F32).astype(BF16)
-        target_send[o] = jnp.dot(teacher[...], pick[pl.ds(0, 1536), :], preferred_element_type=F32).astype(BF16)
+    chan = chan_ref[...]
+    block = blocks_of(chan, 384, 16)
+    block_hits = jnp.concatenate([jnp.where(block == s, 1.0, 0.0) for s in range(16)], axis=0)
+    block_ranks = ranks_of(block_hits, 32) * block_hits
+    rank = block_ranks[0:32, :]
+    for s in range(1, 16):
+        rank += block_ranks[32 * s : 32 * s + 32, :]
+    rank = rank.astype(jnp.int32)
+    group = blocks_of(block, 4, 4)
+    order = block + core * 3 * (block - group * 5)
+    places[0:32, :] = order * SLOT_ROWS + rank
+    places[32:64, :] = jnp.where(block == dp, rank, -1)
+
+    slots = lax.broadcasted_iota(jnp.int32, (SLOT_ROWS, 128), 0)
+    found = jnp.zeros((SLOT_ROWS, 128), jnp.int32)
+    for r in range(32):
+        found += jnp.where(places[32 + r : 33 + r, :] == slots, chan_ref[r : r + 1, :] - dp * 384 + 1, 0)
+    row = jnp.sum(found.astype(F32), axis=1, keepdims=True).astype(jnp.int32) - 1
+    hot = jnp.where(lax.broadcasted_iota(jnp.int32, (SLOT_ROWS, 384), 1) == row, 1.0, 0.0).astype(BF16)
+    load_up.wait()
+    kept_rows[...] = jnp.dot(hot, up[...], preferred_element_type=F32).astype(BF16)
+
+    places[64:128, :] = ff_ref[...] - owner * 1536
+    local = places[64:128, :]
+    mine = (local >= 0) & (local < 1536)
+    slot = ranks_of(jnp.where(mine, 1.0, 0.0), 8).astype(jnp.int32)
+    places[128:192, :] = jnp.where(mine, slot, -1)
+
+    def make_pick(o, carry):
+        slots = lax.broadcasted_iota(jnp.int32, (SLOT_COLS, 128), 0)
+        found = jnp.zeros((SLOT_COLS, 128), jnp.int32)
+        for r in range(8):
+            found += jnp.where(
+                places[pl.ds(128 + o * 8 + r, 1), :] == slots, places[pl.ds(64 + o * 8 + r, 1), :] + 1, 0
+            )
+        column = jnp.sum(found.astype(F32), axis=1, keepdims=True).astype(jnp.int32) - 1
+        hot = jnp.where(lax.broadcasted_iota(jnp.int32, (SLOT_COLS, 1536), 1) == column, 1.0, 0.0)
+        picks[pl.ds(pl.multiple_of(o * 256, 256), 256), :] = hot.astype(BF16)
         return carry
 
-    lax.fori_loop(0, 8, pack, 0)
-    pl.semaphore_wait(barrier, 11)
+    lax.fori_loop(0, 8, make_pick, 0)
+
+    def picked(rows, o):
+        pick = picks[pl.ds(pl.multiple_of(o * 256, 256), 256), :]
+        return lax.dot_general(
+            rows, pick, (((1,), (1,)), ((), ())), preferred_element_type=F32
+        ).astype(BF16)
 
     def weight_copy(k, h):
         peer = (owner + k) % 8
@@ -98,19 +140,46 @@
             device_id_type=MESH,
         )
 
+    pl.semaphore_wait(barrier, 11)
     for h in range(2):
         for k in (4, 3, 5, 2, 6, 1, 7):
+            peer = (owner + k) % 8
+            weight_send[peer, pl.ds(h * 160, 160), :] = picked(kept_rows[h * 160 : h * 160 + 160, :], peer)
             weight_copy(k, h).start()
-    weight_recv[owner] = weight_send[owner]
-    target_recv[owner] = target_send[owner]
+    weight_recv[owner] = picked(kept_rows[...], owner)
+
+    own = ff_ref[pl.ds(pl.multiple_of(owner * 8, 8), 8), :]
+    source = blocks_of(own, 1536, 8)
+    source_hits = jnp.concatenate([jnp.where(source == s, 1.0, 0.0) for s in range(8)], axis=0)
+    source_ranks = ranks_of(source_hits, 8) * source_hits
+    arrives = source * SLOT_COLS
+    for s in range(8):
+        arrives += source_ranks[8 * s : 8 * s + 8, :].astype(jnp.int32)
+    places[192:200, :] = arrives
 
     def make_unpack(s, carry):
-        unpack[pl.ds(pl.multiple_of(s * 256, 256), 256), :] = (
-            lax.broadcasted_iota(jnp.int32, (256, 1024), 0) + s * 256 == from_ref[...]
-        ).astype(F32).astype(BF16)
+        slots = lax.broadcasted_iota(jnp.int32, (256, 128), 0) + s * 256
+        for r in range(8):
+            hot = jnp.where(places[192 + r : 193 + r, :] == slots, 1.0, 0.0)
+            unpack[pl.ds(pl.multiple_of(s * 256, 256), 256), r * 128 : r * 128 + 128] = hot.astype(BF16)
         return carry
 
     lax.fori_loop(0, 8, make_unpack, 0)
+
+    old = gain_ref[...]
+    first = old.astype(BF16)
+    second = (old - first.astype(F32)).astype(BF16)
+    third = (old - first.astype(F32) - second.astype(F32)).astype(BF16)
+    gains = jnp.concatenate([first.astype(F32), second.astype(F32), third.astype(F32)], axis=0).astype(BF16)
+    for r in range(32):
+        line = chan_ref[r : r + 1, :]
+        high = blocks_of(line, 128, 48)
+        low = line - high * 128
+        hot = jnp.where(lax.broadcasted_iota(jnp.int32, (128, 128), 0) == low, 1.0, 0.0).astype(BF16)
+        wide = jnp.dot(gains, hot, preferred_element_type=F32)
+        wide = (wide[0:48, :] + wide[48:96, :]) + wide[96:144, :]
+        chosen = lax.broadcasted_iota(jnp.int32, (48, 128), 0) == high
+        gain[:, r * 128 : r * 128 + 128] = jnp.sum(jnp.where(chosen, wide, 0.0), axis=0, keepdims=True)
     load_tokens.wait()
 
     def norm(r, carry):
@@ -118,7 +187,7 @@
         values = packed_x[rows, pl.ds(0, 4096)].astype(F32)
         center = jnp.mean(values, axis=1, keepdims=True)
         spread = jnp.mean((values - center) ** 2, axis=1, keepdims=True)
-        normed[rows, :] = ((values - center) * lax.rsqrt(spread + 1e-05) * gain_ref[...]).astype(BF16)
+        normed[rows, :] = ((values - center) * lax.rsqrt(spread + 1e-05) * gain[...]).astype(BF16)
         return carry
 
     def slot_row(ao, bo, h):
@@ -160,7 +229,12 @@
             device_id_type=MESH,
         ).wait_recv()
 
-    lax.fori_loop(0, 16, norm, 0)
+    lax.fori_loop(0, 32, norm, 0)
+    load_teacher.wait()
+    target_recv[owner] = picked(teacher[...], owner)
+    for k in (4, 3, 5, 2, 6, 1, 7):
+        peer = (owner + k) % 8
+        target_send[peer] = picked(teacher[...], peer)
     for h in range(2):
         for k in range(1, 8):
             source = (owner - k + 8) % 8
@@ -185,25 +259,30 @@
                 ag_start(ring, step, 0, 0, h)
     for k in (4, 3, 5, 2, 6, 1, 7):
         target_copy(k).start()
-    lax.fori_loop(16, 32, norm, 0)
 
     def permute(c, carry):
         start = pl.multiple_of(c * 256, 256)
-        lanes = lax.broadcasted_iota(jnp.int32, (4096, 128), 1) + start
-        pick[:, pl.ds(0, 128)] = (places[...] == lanes).astype(F32).astype(BF16)
-        pick[:, pl.ds(128, 128)] = (places[...] == lanes + 128).astype(F32).astype(BF16)
-        packed_x[:, pl.ds(start, 256)] = jnp.dot(normed[...], pick[...], preferred_element_type=F32).astype(BF16)
+        slots = lax.broadcasted_iota(jnp.int32, (256, 128), 0) + start
+        total = jnp.zeros((512, 256), F32)
+        for part in range(4):
+            hot = jnp.concatenate(
+                [
+                    jnp.where(places[r : r + 1, :] == slots, 1.0, 0.0).astype(BF16)
+                    for r in range(part * 8, part * 8 + 8)
+                ],
+                axis=1,
+            )
+            total += lax.dot_general(
+                normed[:, part * 1024 : part * 1024 + 1024], hot, (((1,), (1,)), ((), ())), preferred_element_type=F32
+            )
+        packed_x[:, pl.ds(start, 256)] = total.astype(BF16)
         return carry
 
-    def permute_group(bo):
-        first = ((b + bo) % 4) * 5
-        lax.fori_loop(first, first + 5, permute, 0)
-
-    def transpose(ao, bo):
-        aa, bb = (a + ao) % 4, (b + bo) % 4
-        cols = pl.ds(pl.multiple_of(dp_of(ao, bo) * 256, 256), 256)
-        rows = pl.ds(pl.multiple_of((aa * 4 + bb) * 256, 256), 256)
-        normed_t[rows, :] = normed[:, cols].T
+    def fill(first, last):
+        def one(q, carry):
+            return permute((b * 5 + q) % 20, carry)
+
+        lax.fori_loop(first, last, one, 0)
 
     def multiply_group(bo, first):
         depth = pl.ds(pl.multiple_of(((b + bo) % 4) * 1280, 256), 1280)
@@ -214,38 +293,41 @@
             part = jnp.dot(packed_x[:, depth], weights[depth, cols], preferred_element_type=F32)
             pre[:, cols] = part if first else pre[:, cols] + part
 
-    load_places.wait()
-
-    for ao, h in ((3, 0), (1, 1), (3, 1), (1, 0)):
-        ag_wait(0, ao, 0, h)
-        if (ao, h) == (3, 0):
-            ag_start(0, 1, 3, 0, 0)
-        if (ao, h) == (1, 1):
-            ag_start(0, 3, 1, 0, 1)
-        ag_start(1, 1, ao, 0, h)
-        ag_start(1, 3, ao, 0, h)
-    ag_wait(1, 0, 3, 0)
-    ag_start(1, 1, 0, 3, 0)
-    ag_wait(1, 0, 1, 1)
-    ag_start(1, 3, 0, 1, 1)
-    for h in range(2):
-        ag_wait(0, 2, 0, h)
-        ag_start(1, 1, 2, 0, h)
-        ag_start(1, 3, 2, 0, h)
-    permute_group(0)
-    for ao in (3, 1):
-        ag_wait(1, ao, 3, 0)
-        ag_start(1, 1, ao, 3, 0)
-        ag_wait(1, ao, 1, 1)
-        ag_start(1, 3, ao, 1, 1)
-    permute_group(3)
-    ag_wait(1, 2, 3, 0)
-    ag_start(1, 1, 2, 3, 0)
-    ag_wait(1, 2, 1, 1)
-    ag_start(1, 3, 2, 1, 1)
+    def relay(ring, ao, bo, h):
+        ag_wait(ring, ao, bo, h)
+        far = ao if ring == 0 else bo
+        if far == 3 and h == 0:
+            ag_start(ring, 1, ao, bo, h)
+        if far == 1 and h == 1:
+            ag_start(ring, 3, ao, bo, h)
+        if ring == 0:
+            ag_start(1, 1, ao, 0, h)
+            ag_start(1, 3, ao, 0, h)
+
+    relay(0, 3, 0, 0)
+    relay(0, 1, 0, 0)
+    relay(1, 0, 3, 0)
+    fill(0, 2)
+    relay(0, 1, 0, 1)
+    relay(0, 3, 0, 1)
+    relay(1, 0, 1, 1)
+    fill(2, 4)
+    relay(0, 2, 0, 0)
+    fill(4, 5)
+    relay(0, 2, 0, 1)
+    relay(1, 3, 3, 0)
+    fill(5, 6)
+    relay(1, 3, 1, 1)
+    fill(6, 7)
+    relay(1, 1, 3, 0)
+    fill(7, 8)
+    relay(1, 1, 1, 1)
+    fill(8, 9)
+    relay(1, 2, 3, 0)
+    fill(9, 10)
+    relay(1, 2, 1, 1)
+    fill(10, 20)
     multiply_group(0, True)
-    permute_group(1)
-    permute_group(2)
 
     @pl.loop(0, 16)
     def _(s):
@@ -401,46 +483,7 @@
 
 
 def per_device(tokens_in, teacher_hidden, up_old, gain_old, keep_chan, keep_ff):
-    dp = lax.axis_index("dp")
-    owner = lax.axis_index("tensor")
-    core = owner % 2
     scale = 1.0 / math.sqrt(tokens_in.shape[0] * lax.axis_size("dp"))
-
-    blocks = keep_ff.reshape(8, 1024)
-    local = blocks - owner * 1536
-    mine = (local >= 0) & (local < 1536)
-    slot = jnp.where(mine, ranks_of(mine), -1)
-    cols = jnp.sum(
-        jnp.where(slot[:, None, :] == jnp.arange(SLOT_COLS)[None, :, None], local[:, None, :] + 1, 0), axis=2
-    ) - 1
-
-    own = lax.dynamic_slice_in_dim(keep_ff, owner * 1024, 1024)
-    source_hits = own[None, :] // 1536 == jnp.arange(8)[:, None]
-    where_from = jnp.sum(
-        jnp.where(source_hits, ranks_of(source_hits) + jnp.arange(8)[:, None] * SLOT_COLS, 0), axis=0
-    )
-
-    block = keep_chan // 384
-    block_hits = block[None, :] == jnp.arange(16)[:, None]
-    rank = jnp.sum(jnp.where(block_hits, ranks_of(block_hits), 0), axis=0)
-    turned = (block % 4) * 4 + block // 4
-    order = jnp.where(core == 0, block, turned)
-    pos = order * SLOT_ROWS + rank
-    pos = jnp.broadcast_to(pos[:, None], (4096, 128))
-    rank_here = jnp.where(block == dp, rank, -1)
-    rowsel = jnp.sum(
-        jnp.where(rank_here[None, :] == jnp.arange(SLOT_ROWS)[:, None], keep_chan[None, :] - dp * 384 + 1, 0),
-        axis=1, keepdims=True,
-    ) - 1
-
-    high = (keep_chan[None, :] // 128 == jnp.arange(48)[:, None]).astype(F32)
-    low = keep_chan[None, :] % 128 == jnp.arange(128)[:, None]
-    wide = lax.dot_general(
-        gain_old.reshape(48, 128), high, (((0,), (0,)), ((), ())),
-        precision=lax.Precision.HIGHEST, preferred_element_type=F32,
-    )
-    gain = jnp.sum(jnp.where(low, wide, 0.0), axis=0, keepdims=True)
-
     anywhere = pl.BlockSpec(memory_space=pl.ANY)
     vmem = pl.BlockSpec(memory_space=pltpu.VMEM)
     dma = pltpu.SemaphoreType.DMA
@@ -451,7 +494,7 @@
     return pl.pallas_call(
         body,
         out_shape=jax.ShapeDtypeStruct((256, 1024), F32),
-        in_specs=[anywhere, anywhere, vmem, vmem, vmem, vmem, vmem, anywhere],
+        in_specs=[anywhere, anywhere, anywhere, vmem, vmem, vmem],
         out_specs=vmem,
         scratch_shapes=[
             pltpu.VMEM((512, 4096), BF16),
@@ -459,19 +502,21 @@
             pltpu.VMEM((512, 5120), BF16),
             pltpu.VMEM((5120, 1024), BF16),
             pltpu.VMEM((512, 1536), BF16),
+            pltpu.VMEM((384, 1536), BF16),
             pltpu.VMEM((SLOT_ROWS, 1536), BF16),
             pltpu.VMEM((8, SLOT_ROWS, SLOT_COLS), BF16),
             pltpu.VMEM((8, SLOT_ROWS, SLOT_COLS), BF16),
             pltpu.VMEM((8, 512, SLOT_COLS), BF16),
             pltpu.VMEM((8, 512, SLOT_COLS), BF16),
             pltpu.VMEM((2048, 1024), BF16),
-            pltpu.VMEM((4096, 128), jnp.int32),
-            pltpu.VMEM((4096, 256), BF16),
+            pltpu.VMEM((2048, 1536), BF16),
             pltpu.VMEM((512, 1024), F32),
             pltpu.VMEM((512, 1024), BF16),
             pltpu.VMEM((512, 1024), BF16),
             pltpu.VMEM((24 * 128, 1024), BF16),
             pltpu.VMEM((6 * 128, 1024), BF16),
+            pltpu.VMEM((1, 4096), F32),
+            pltpu.VMEM((200, 128), jnp.int32),
             dma((3,)),
             dma((16,)),
             dma((16,)),
@@ -486,7 +531,10 @@
             collective_id=0, has_side_effects=True, vmem_limit_bytes=62 * 1024 * 1024
         ),
         cost_estimate=pl.CostEstimate(flops=40_000_000_000, bytes_accessed=10_000_000, transcendentals=0),
-    )(tokens_in, teacher_hidden, up_old, gain, cols, rowsel, where_from[None, :], pos)
+    )(
+        tokens_in, teacher_hidden, up_old,
+        gain_old.reshape(48, 128), keep_chan.reshape(32, 128), keep_ff.reshape(64, 128),
+    )
 
 
 def solution(mesh):

time: 164 us -> 158 us (0.963)
  Pallas kernels: 148 us -> 156 us
  other arithmetic: 6.48 us -> 0 us
  local copies, waits for them, and re-layouts: 6.04 us -> 2.31 us
  matrix products: 3.2 us -> 0 us
    pallas_call x1, Pallas kernels: 148 us -> 156 us  [per_device(): pl.pallas_call(body, out_shape=jax.ShapeDtypeStruct((256, 1024), F32), in...]
    dot_general x7 -> x0, matrix products: 3.2 us -> none  [the longest x1 1.78 us: per_device(): lax.dot_general(gain_old.reshape(48, 128), high, (((0,), (0,)), ((), ()))...]
    broadcast_in_dim x1 -> x0, local copies, waits for them, and re-layouts: 2.93 us -> none  [per_device(): pos = jnp.broadcast_to(pos[:, None], (4096, 128))]
    reduce_sum x5 -> x0, other arithmetic: 2.84 us -> none  [the longest x3 1.09 us: ranks_of(): jnp.sum(hits.astype(F32).reshape(rows, chunks, 128), axis=2).astype(BF16)]
where the time goes in v2:
time: 158 us
  Pallas kernels  156 us (99%)
  local copies, waits for them, and re-layouts  2.31 us (1%)
    pallas_call x1, Pallas kernels, per_device(): pl.pallas_call(body, out_shape=jax.ShapeDtypeStruct((256, 1024), F32), in...  156 us

profile of v2, /device:TPU:34, one launch (start us, length us, event | category | flops | bytes accessed | tf_op | source)
XLA Modules:
  0.0 158.1 jit_solution(44707063283876150)
XLA Ops:
  0.0 155.8 %shard_map.64 = f32[256,1024]{1,0:T(8,128)} custom-call(bf16[512,4096]{1,0:T(8,128)(2,1)} %refs_0_.1, bf16[512,1536]{1,0:T(8,128)(2,1)} %refs_1_.1, bf16[384,1536]{1,0:T(8,128)(2,1)} %refs_2_.1, f32[48,128]{1,0:T(8,128)} %bitcast.4, s32[32,128]{1,0:T(8,128)} %bitcast.5, s32[64,128]{1,0:T(8,128)} %bitcast.3), custom_call_target="tpu_custom_call" | custom-call | flops 40000000000 | bytes 10000000 | tf_op jit(solution)/shard_map/pallas_call | solution.py:494
  155.8 2.3 %copy.8 = f32[256,1024]{1,0:T(8,128)} copy(f32[256,1024]{1,0:T(8,128)} %shard_map.64) | data formatting | bytes 2097152

commit v3 on v2

--- a/solution.py
+++ b/solution.py
@@ -141,12 +141,13 @@
         )
 
     pl.semaphore_wait(barrier, 11)
-    for h in range(2):
-        for k in (4, 3, 5, 2, 6, 1, 7):
-            peer = (owner + k) % 8
-            weight_send[peer, pl.ds(h * 160, 160), :] = picked(kept_rows[h * 160 : h * 160 + 160, :], peer)
-            weight_copy(k, h).start()
-    weight_recv[owner] = picked(kept_rows[...], owner)
+    for k in (4, 3, 5, 2, 6, 1, 7):
+        peer = (owner + k) % 8
+        weight_send[peer] = picked(kept_rows[...], peer)
+        weight_copy(k, 0).start()
+    for k in (4, 3, 5, 2, 6, 1, 7):
+        weight_copy(k, 1).start()
+    weight_send[owner] = picked(kept_rows[...], owner)
 
     own = ff_ref[pl.ds(pl.multiple_of(owner * 8, 8), 8), :]
     source = blocks_of(own, 1536, 8)
@@ -236,24 +237,23 @@
         peer = (owner + k) % 8
         target_send[peer] = picked(teacher[...], peer)
     for h in range(2):
-        for k in range(1, 8):
+        half = pl.ds(h * 160, 160)
+        for k in (0, 4, 3, 5, 2, 6, 1, 7):
             source = (owner - k + 8) % 8
+            table = unpack[pl.ds(pl.multiple_of(source * 256, 256), 256), :]
+            if k == 0:
+                pre[half, :] = jnp.dot(weight_send[owner, half, :], table, preferred_element_type=F32)
+                continue
             pltpu.make_async_remote_copy(
-                src_ref=weight_recv.at[source, pl.ds(h * 160, 160), :],
-                dst_ref=weight_recv.at[source, pl.ds(h * 160, 160), :],
+                src_ref=weight_recv.at[source, half, :],
+                dst_ref=weight_recv.at[source, half, :],
                 send_sem=ws_send.at[h * 8 + k],
                 recv_sem=ws_recv.at[h * 8 + k],
                 device_id=(dp, (owner + k) % 8),
                 device_id_type=MESH,
             ).wait_recv()
-        total = jnp.zeros((160, 1024), F32)
-        for s in range(8):
-            total += jnp.dot(
-                weight_recv[s, h * 160 : h * 160 + 160, :],
-                unpack[s * 256 : s * 256 + 256, :],
-                preferred_element_type=F32,
-            )
-        weights[pl.ds(slot_row(0, 0, h), 160), :] = total.astype(BF16)
+            pre[half, :] += jnp.dot(weight_recv[source, half, :], table, preferred_element_type=F32)
+        weights[pl.ds(slot_row(0, 0, h), 160), :] = pre[half, :].astype(BF16)
         for ring in (0, 1):
             for step in (1, 3):
                 ag_start(ring, step, 0, 0, h)
@@ -304,30 +304,28 @@
             ag_start(1, 1, ao, 0, h)
             ag_start(1, 3, ao, 0, h)
 
+    fill(0, 4)
     relay(0, 3, 0, 0)
     relay(0, 1, 0, 0)
     relay(1, 0, 3, 0)
-    fill(0, 2)
+    fill(4, 8)
     relay(0, 1, 0, 1)
     relay(0, 3, 0, 1)
     relay(1, 0, 1, 1)
-    fill(2, 4)
+    fill(8, 11)
     relay(0, 2, 0, 0)
-    fill(4, 5)
+    fill(11, 13)
     relay(0, 2, 0, 1)
     relay(1, 3, 3, 0)
-    fill(5, 6)
+    fill(13, 15)
     relay(1, 3, 1, 1)
-    fill(6, 7)
     relay(1, 1, 3, 0)
-    fill(7, 8)
+    fill(15, 17)
     relay(1, 1, 1, 1)
-    fill(8, 9)
+    fill(17, 20)
     relay(1, 2, 3, 0)
-    fill(9, 10)
+    multiply_group(0, True)
     relay(1, 2, 1, 1)
-    fill(10, 20)
-    multiply_group(0, True)
 
     @pl.loop(0, 16)
     def _(s):

time: 158 us -> 143 us (0.905)
  Pallas kernels: 156 us -> 141 us
    pallas_call x1, Pallas kernels: 156 us -> 141 us  [per_device(): pl.pallas_call(body, out_shape=jax.ShapeDtypeStruct((256, 1024), F32), in...]
where the time goes in v3:
time: 143 us
  Pallas kernels  141 us (99%)
  local copies, waits for them, and re-layouts  2.31 us (2%)
    pallas_call x1, Pallas kernels, per_device(): pl.pallas_call(body, out_shape=jax.ShapeDtypeStruct((256, 1024), F32), in...  141 us

profile of v3, /device:TPU:34, one launch (start us, length us, event | category | flops | bytes accessed | tf_op | source)
XLA Modules:
  0.0 142.9 jit_solution(6962513111092829826)
XLA Ops:
  0.0 140.6 %shard_map.64 = f32[256,1024]{1,0:T(8,128)} custom-call(bf16[512,4096]{1,0:T(8,128)(2,1)} %refs_0_.1, bf16[512,1536]{1,0:T(8,128)(2,1)} %refs_1_.1, bf16[384,1536]{1,0:T(8,128)(2,1)} %refs_2_.1, f32[48,128]{1,0:T(8,128)} %bitcast.4, s32[32,128]{1,0:T(8,128)} %bitcast.5, s32[64,128]{1,0:T(8,128)} %bitcast.3), custom_call_target="tpu_custom_call" | custom-call | flops 40000000000 | bytes 10000000 | tf_op jit(solution)/shard_map/pallas_call | solution.py:492
  140.6 2.3 %copy.8 = f32[256,1024]{1,0:T(8,128)} copy(f32[256,1024]{1,0:T(8,128)} %shard_map.64) | data formatting | bytes 2097152

commit v4 on v3

--- a/solution.py
+++ b/solution.py
@@ -42,7 +42,7 @@
     out_ref,
     normed, normed_t, packed_x, weights, teacher, up, kept_rows, weight_send, weight_recv,
     target_send, target_recv, unpack, picks, pre, delta, target, ring_b, ring_a, gain, places,
-    local_sems, ws_send, ws_recv, ts_send, ts_recv, ag_send, ag_recv, rs_send, rs_recv,
+    local_sems, ws_send, ws_recv, ts_send, ts_recv, ag_send, ag_recv, rs_send, rs_recv, px_send, px_recv,
 ):
     dp = lax.axis_index("dp")
     owner = lax.axis_index("tensor")
@@ -60,7 +60,7 @@
 
     load_up = pltpu.make_async_copy(up_hbm, up, local_sems.at[0])
     load_teacher = pltpu.make_async_copy(teacher_hbm, teacher, local_sems.at[1])
-    load_tokens = pltpu.make_async_copy(tokens_hbm, packed_x.at[:, pl.ds(0, 4096)], local_sems.at[2])
+    load_tokens = pltpu.make_async_copy(tokens_hbm, normed, local_sems.at[2])
     load_up.start()
     load_teacher.start()
     load_tokens.start()
@@ -78,9 +78,7 @@
     for s in range(1, 16):
         rank += block_ranks[32 * s : 32 * s + 32, :]
     rank = rank.astype(jnp.int32)
-    group = blocks_of(block, 4, 4)
-    order = block + core * 3 * (block - group * 5)
-    places[0:32, :] = order * SLOT_ROWS + rank
+    places[0:32, :] = block * SLOT_ROWS + rank
     places[32:64, :] = jnp.where(block == dp, rank, -1)
 
     slots = lax.broadcasted_iota(jnp.int32, (SLOT_ROWS, 128), 0)
@@ -181,19 +179,16 @@
         wide = (wide[0:48, :] + wide[48:96, :]) + wide[96:144, :]
         chosen = lax.broadcasted_iota(jnp.int32, (48, 128), 0) == high
         gain[:, r * 128 : r * 128 + 128] = jnp.sum(jnp.where(chosen, wide, 0.0), axis=0, keepdims=True)
-    load_tokens.wait()
-
     def norm(r, carry):
-        rows = pl.ds(pl.multiple_of(r * 16, 16), 16)
-        values = packed_x[rows, pl.ds(0, 4096)].astype(F32)
+        rows = pl.ds(pl.multiple_of(r * 32, 32), 32)
+        values = normed[rows, :].astype(F32)
         center = jnp.mean(values, axis=1, keepdims=True)
         spread = jnp.mean((values - center) ** 2, axis=1, keepdims=True)
         normed[rows, :] = ((values - center) * lax.rsqrt(spread + 1e-05) * gain[...]).astype(BF16)
         return carry
 
     def slot_row(ao, bo, h):
-        aa, bb = (a + ao) % 4, (b + bo) % 4
-        return pl.multiple_of((bb * 4 + aa) * SLOT_ROWS + h * 160, 32)
+        return pl.multiple_of(dp_of(ao, bo) * SLOT_ROWS + h * 160, 32)
 
     ag_started = []
 
@@ -230,12 +225,12 @@
             device_id_type=MESH,
         ).wait_recv()
 
-    lax.fori_loop(0, 32, norm, 0)
     load_teacher.wait()
     target_recv[owner] = picked(teacher[...], owner)
     for k in (4, 3, 5, 2, 6, 1, 7):
         peer = (owner + k) % 8
         target_send[peer] = picked(teacher[...], peer)
+    load_tokens.wait()
     for h in range(2):
         half = pl.ds(h * 160, 160)
         for k in (0, 4, 3, 5, 2, 6, 1, 7):
@@ -257,12 +252,23 @@
         for ring in (0, 1):
             for step in (1, 3):
                 ag_start(ring, step, 0, 0, h)
+        lax.fori_loop(h * 8, h * 8 + 8, norm, 0)
     for k in (4, 3, 5, 2, 6, 1, 7):
         target_copy(k).start()
 
-    def permute(c, carry):
-        start = pl.multiple_of(c * 256, 256)
-        slots = lax.broadcasted_iota(jnp.int32, (256, 128), 0) + start
+    def chunk_copy(index, turn):
+        return pltpu.make_async_remote_copy(
+            src_ref=packed_x.at[index],
+            dst_ref=packed_x.at[index],
+            send_sem=px_send.at[turn],
+            recv_sem=px_recv.at[turn],
+            device_id=(dp, owner + 1 - 2 * core),
+            device_id_type=MESH,
+        )
+
+    def permute(turn, carry):
+        index = (z * 5 + 2 * turn + core) % 20
+        slots = lax.broadcasted_iota(jnp.int32, (256, 128), 0) + index * 256
         total = jnp.zeros((512, 256), F32)
         for part in range(4):
             hot = jnp.concatenate(
@@ -275,23 +281,29 @@
             total += lax.dot_general(
                 normed[:, part * 1024 : part * 1024 + 1024], hot, (((1,), (1,)), ((), ())), preferred_element_type=F32
             )
-        packed_x[:, pl.ds(start, 256)] = total.astype(BF16)
+        packed_x[index] = total.astype(BF16)
+        chunk_copy(index, turn).start()
         return carry
 
     def fill(first, last):
-        def one(q, carry):
-            return permute((b * 5 + q) % 20, carry)
-
-        lax.fori_loop(first, last, one, 0)
-
-    def multiply_group(bo, first):
-        depth = pl.ds(pl.multiple_of(((b + bo) % 4) * 1280, 256), 1280)
-
-        @pl.loop(0, 4)
+        lax.fori_loop(first, last, permute, 0)
+
+    def take_chunks(first, last):
+        @pl.loop(first, last)
+        def _(turn):
+            chunk_copy((z * 5 + 2 * turn + 1 - core) % 20, turn).wait_recv()
+
+    def multiply_group(zo, first):
+        base = ((z + zo) % 4) * 5
+
+        @pl.loop(0, 2)
         def _(n):
-            cols = pl.ds(pl.multiple_of(n * 256, 256), 256)
-            part = jnp.dot(packed_x[:, depth], weights[depth, cols], preferred_element_type=F32)
-            pre[:, cols] = part if first else pre[:, cols] + part
+            cols = pl.ds(pl.multiple_of(n * 512, 512), 512)
+            part = jnp.zeros((512, 512), F32) if first else pre[:, cols]
+            for c in range(5):
+                depth = pl.ds(pl.multiple_of((base + c) * 256, 256), 256)
+                part += jnp.dot(packed_x[base + c], weights[depth, cols], preferred_element_type=F32)
+            pre[:, cols] = part
 
     def relay(ring, ao, bo, h):
         ag_wait(ring, ao, bo, h)
@@ -304,34 +316,33 @@
             ag_start(1, 1, ao, 0, h)
             ag_start(1, 3, ao, 0, h)
 
-    fill(0, 4)
     relay(0, 3, 0, 0)
     relay(0, 1, 0, 0)
     relay(1, 0, 3, 0)
-    fill(4, 8)
+    fill(0, 2)
     relay(0, 1, 0, 1)
     relay(0, 3, 0, 1)
     relay(1, 0, 1, 1)
-    fill(8, 11)
+    fill(2, 4)
     relay(0, 2, 0, 0)
-    fill(11, 13)
+    fill(4, 6)
     relay(0, 2, 0, 1)
     relay(1, 3, 3, 0)
-    fill(13, 15)
+    fill(6, 7)
     relay(1, 3, 1, 1)
     relay(1, 1, 3, 0)
-    fill(15, 17)
+    fill(7, 8)
     relay(1, 1, 1, 1)
-    fill(17, 20)
+    fill(8, 10)
     relay(1, 2, 3, 0)
-    multiply_group(0, True)
-    relay(1, 2, 1, 1)
 
     @pl.loop(0, 16)
     def _(s):
         aa, bb = s // 4, s % 4
         cols = pl.ds(pl.multiple_of((bb * 4 + aa + core * 3 * (aa - bb)) * 256, 256), 256)
         normed_t[pl.ds(pl.multiple_of(s * 256, 256), 256), :] = normed[:, cols].T
+
+    relay(1, 2, 1, 1)
 
     for k in range(1, 8):
         source = (owner - k + 8) % 8
@@ -352,14 +363,23 @@
             total += jnp.dot(target_recv[s], unpack[s * 256 : s * 256 + 256, cols], preferred_element_type=F32)
         target[:, cols] = total.astype(BF16)
 
-    for ao in range(4):
+    take_chunks(0, 10)
+    for bo, h in ((3, 1), (1, 0), (2, 0), (2, 1)):
+        ag_wait(1, 0, bo, h)
+    multiply_group(0, True)
+    for ao in (3, 1, 2):
         ag_wait(1, ao, 3, 1)
+    for h in range(2):
+        ag_wait(1, 3, 2, h)
+    ag_wait(1, 3, 1, 0)
+    multiply_group(3, False)
+    for ao in (1, 2):
         ag_wait(1, ao, 1, 0)
-    multiply_group(3, False)
+    for h in range(2):
+        ag_wait(1, 1, 2, h)
     multiply_group(1, False)
-    for ao in range(4):
-        ag_wait(1, ao, 2, 0)
-        ag_wait(1, ao, 2, 1)
+    for h in range(2):
+        ag_wait(1, 2, 2, h)
     multiply_group(2, False)
 
     @pl.loop(0, 32)
@@ -374,6 +394,10 @@
         for h in range(2):
             weight_copy(k, h).wait_send()
         target_copy(k).wait_send()
+
+    @pl.loop(0, 10)
+    def _(turn):
+        chunk_copy((z * 5 + 2 * turn + core) % 20, turn).wait_send()
 
     rs_started = []
 
@@ -497,7 +521,7 @@
         scratch_shapes=[
             pltpu.VMEM((512, 4096), BF16),
             pltpu.VMEM((4096, 512), BF16),
-            pltpu.VMEM((512, 5120), BF16),
+            pltpu.VMEM((20, 512, 256), BF16),
             pltpu.VMEM((5120, 1024), BF16),
             pltpu.VMEM((512, 1536), BF16),
             pltpu.VMEM((384, 1536), BF16),
@@ -524,6 +548,8 @@
             dma((30,)),
             dma((30,)),
             dma((30,)),
+            dma((10,)),
+            dma((10,)),
         ],
         compiler_params=pltpu.CompilerParams(
             collective_id=0, has_side_effects=True, vmem_limit_bytes=62 * 1024 * 1024

time: 143 us -> 135 us (0.944)
  Pallas kernels: 141 us -> 132 us
    pallas_call x1, Pallas kernels: 141 us -> 132 us  [per_device(): pl.pallas_call(body, out_shape=jax.ShapeDtypeStruct((256, 1024), F32), in...]
where the time goes in v4:
time: 135 us
  Pallas kernels  132 us (98%)
  local copies, waits for them, and re-layouts  2.31 us (2%)
    pallas_call x1, Pallas kernels, per_device(): pl.pallas_call(body, out_shape=jax.ShapeDtypeStruct((256, 1024), F32), in...  132 us

profile of v4, /device:TPU:34, one launch (start us, length us, event | category | flops | bytes accessed | tf_op | source)
XLA Modules:
  0.0 134.8 jit_solution(17455403874704688953)
XLA Ops:
  0.0 132.5 %shard_map.64 = f32[256,1024]{1,0:T(8,128)} custom-call(bf16[512,4096]{1,0:T(8,128)(2,1)} %refs_0_.1, bf16[512,1536]{1,0:T(8,128)(2,1)} %refs_1_.1, bf16[384,1536]{1,0:T(8,128)(2,1)} %refs_2_.1, f32[48,128]{1,0:T(8,128)} %bitcast.4, s32[32,128]{1,0:T(8,128)} %bitcast.5, s32[64,128]{1,0:T(8,128)} %bitcast.3), custom_call_target="tpu_custom_call" | custom-call | flops 40000000000 | bytes 10000000 | tf_op jit(solution)/shard_map/pallas_call | solution.py:516
  132.5 2.3 %copy.8 = f32[256,1024]{1,0:T(8,128)} copy(f32[256,1024]{1,0:T(8,128)} %shard_map.64) | data formatting | bytes 2097152

commit v5 on v4

--- a/solution.py
+++ b/solution.py
@@ -108,8 +108,6 @@
         picks[pl.ds(pl.multiple_of(o * 256, 256), 256), :] = hot.astype(BF16)
         return carry
 
-    lax.fori_loop(0, 8, make_pick, 0)
-
     def picked(rows, o):
         pick = picks[pl.ds(pl.multiple_of(o * 256, 256), 256), :]
         return lax.dot_general(
@@ -139,12 +137,19 @@
         )
 
     pl.semaphore_wait(barrier, 11)
-    for k in (4, 3, 5, 2, 6, 1, 7):
+
+    def pack(i, carry):
+        k = 4 + (i + 1) // 2 * (1 - 2 * (i % 2))
         peer = (owner + k) % 8
+        make_pick(peer, carry)
         weight_send[peer] = picked(kept_rows[...], peer)
         weight_copy(k, 0).start()
+        return carry
+
+    lax.fori_loop(0, 7, pack, 0)
     for k in (4, 3, 5, 2, 6, 1, 7):
         weight_copy(k, 1).start()
+    make_pick(owner, 0)
     weight_send[owner] = picked(kept_rows[...], owner)
 
     own = ff_ref[pl.ds(pl.multiple_of(owner * 8, 8), 8), :]
@@ -445,8 +450,9 @@
             else:
                 weights[pl.ds(base + r * 16, 16), :] = total.astype(BF16)
 
-    def products(ao):
-        rows = pl.ds(pl.multiple_of(((a + ao) % 4) * 1024, 1024), 1024)
+    def products(ao, bo, count):
+        first = ((a + ao) % 4) * 4 + (b + bo) % 4 if count == 1 else ((a + ao) % 4) * 4
+        rows = pl.ds(pl.multiple_of(first * 256, 256), 256 * count)
 
         @pl.loop(0, 4)
         def _(n):
@@ -455,11 +461,14 @@
                 normed_t[rows, :], delta[:, cols], preferred_element_type=F32
             ).astype(BF16)
 
-    def spread_b(ao):
-        rs_start(1, 1, ao, 2, 0, 0)
-        rs_start(1, 3, ao, 2, 1, 1)
-        rs_start(1, 1, ao, 1, 1, 3)
-        rs_start(1, 3, ao, 3, 0, 4)
+    def spread_b(ao, only=None):
+        if only in (None, 2):
+            rs_start(1, 1, ao, 2, 0, 0)
+            rs_start(1, 3, ao, 2, 1, 1)
+        if only in (None, 1):
+            rs_start(1, 1, ao, 1, 1, 3)
+        if only in (None, 3):
+            rs_start(1, 3, ao, 3, 0, 4)
 
     def relay_b(ao):
         add_into(ao, 1, 0, [rs_take(1, ao, 0)])
@@ -471,29 +480,31 @@
         for h in range(2):
             add_into(ao, 0, h, [rs_take(1, ao, 2 + h), rs_take(1, ao, 4 + h)])
 
-    products(2)
-    spread_b(2)
-    products(1)
+    for bo in (2, 1, 3):
+        products(2, bo, 1)
+        spread_b(2, bo)
+    products(1, 0, 4)
     spread_b(1)
+    products(3, 0, 4)
+    spread_b(3)
     relay_b(2)
-    products(3)
-    spread_b(3)
     relay_b(1)
-    products(0)
+    relay_b(3)
+    products(0, 0, 4)
     spread_b(0)
-    relay_b(3)
+    products(2, 0, 1)
     gather_b(2)
     rs_start(0, 1, 2, 0, 0, 0)
     rs_start(0, 3, 2, 0, 1, 1)
-    relay_b(0)
     gather_b(1)
     rs_start(0, 1, 1, 0, 1, 3)
+    gather_b(3)
+    rs_start(0, 3, 3, 0, 0, 4)
     add_into(1, 0, 0, [rs_take(0, 0, 0)])
     rs_start(0, 1, 1, 0, 0, 2)
-    gather_b(3)
-    rs_start(0, 3, 3, 0, 0, 4)
     add_into(3, 0, 1, [rs_take(0, 0, 1)])
     rs_start(0, 3, 3, 0, 1, 5)
+    relay_b(0)
     for h in range(2):
         add_into(
             0, 0, h,

time: 135 us -> 129 us (0.956)
  Pallas kernels: 132 us -> 125 us
    pallas_call x1, Pallas kernels: 132 us -> 125 us  [per_device(): pl.pallas_call(body, out_shape=jax.ShapeDtypeStruct((256, 1024), F32), in...]
where the time goes in v5:
time: 129 us; the launch traced here: 128 us
  Pallas kernels  125 us (97%)
  local copies, waits for them, and re-layouts  2.31 us (2%)
    pallas_call x1, Pallas kernels, per_device(): pl.pallas_call(body, out_shape=jax.ShapeDtypeStruct((256, 1024), F32), in...  125 us

profile of v5, /device:TPU:34, one launch (start us, length us, event | category | flops | bytes accessed | tf_op | source)
XLA Modules:
  0.0 127.7 jit_solution(15543060765081847978)
XLA Ops:
  0.0 125.4 %shard_map.64 = f32[256,1024]{1,0:T(8,128)} custom-call(bf16[512,4096]{1,0:T(8,128)(2,1)} %refs_0_.1, bf16[512,1536]{1,0:T(8,128)(2,1)} %refs_1_.1, bf16[384,1536]{1,0:T(8,128)(2,1)} %refs_2_.1, f32[48,128]{1,0:T(8,128)} %bitcast.4, s32[32,128]{1,0:T(8,128)} %bitcast.5, s32[64,128]{1,0:T(8,128)} %bitcast.3), custom_call_target="tpu_custom_call" | custom-call | flops 40000000000 | bytes 10000000 | tf_op jit(solution)/shard_map/pallas_call | solution.py:527
  125.4 2.3 %copy.8 = f32[256,1024]{1,0:T(8,128)} copy(f32[256,1024]{1,0:T(8,128)} %shard_map.64) | data formatting | bytes 2097152

commit v6 on v5

--- a/solution.py
+++ b/solution.py
@@ -10,6 +10,9 @@
 MESH = pl.DeviceIdType.MESH
 SLOT_ROWS = 320
 SLOT_COLS = 256
+PIECES = 4
+SLOT_PIECE = SLOT_ROWS // PIECES
+GRAD_PIECE = 256 // PIECES
 BF16 = jnp.bfloat16
 F32 = jnp.float32
 
@@ -117,8 +120,8 @@
     def weight_copy(k, h):
         peer = (owner + k) % 8
         return pltpu.make_async_remote_copy(
-            src_ref=weight_send.at[peer, pl.ds(h * 160, 160), :],
-            dst_ref=weight_recv.at[owner, pl.ds(h * 160, 160), :],
+            src_ref=weight_send.at[peer, pl.ds(h * SLOT_PIECE, SLOT_PIECE), :],
+            dst_ref=weight_recv.at[owner, pl.ds(h * SLOT_PIECE, SLOT_PIECE), :],
             send_sem=ws_send.at[h * 8 + k],
             recv_sem=ws_recv.at[h * 8 + k],
             device_id=(dp, peer),
@@ -147,8 +150,9 @@
         return carry
 
     lax.fori_loop(0, 7, pack, 0)
-    for k in (4, 3, 5, 2, 6, 1, 7):
-        weight_copy(k, 1).start()
+    for h in range(1, PIECES):
+        for k in (4, 3, 5, 2, 6, 1, 7):
+            weight_copy(k, h).start()
     make_pick(owner, 0)
     weight_send[owner] = picked(kept_rows[...], owner)
 
@@ -193,15 +197,15 @@
         return carry
 
     def slot_row(ao, bo, h):
-        return pl.multiple_of(dp_of(ao, bo) * SLOT_ROWS + h * 160, 32)
+        return pl.multiple_of(dp_of(ao, bo) * SLOT_ROWS + h * SLOT_PIECE, 16)
 
     ag_started = []
 
     def ag_copy(ring, step, ao, bo, h):
         far = (ao if ring == 0 else bo) != 0
-        role = (4 + h) if far else ((0 if step == 1 else 2) + h)
-        index = role if ring == 0 else 6 + ao * 6 + role
-        rows = pl.ds(slot_row(ao, bo, h), 160)
+        role = (2 * PIECES if far else 0 if step == 1 else PIECES) + h
+        index = role if ring == 0 else 3 * PIECES * (1 + ao) + role
+        rows = pl.ds(slot_row(ao, bo, h), SLOT_PIECE)
         return pltpu.make_async_remote_copy(
             src_ref=weights.at[rows, :],
             dst_ref=weights.at[rows, :],
@@ -218,9 +222,9 @@
 
     def ag_wait(ring, ao, bo, h):
         offset = ao if ring == 0 else bo
-        role = {3: 0, 1: 2, 2: 4}[offset] + h
-        index = role if ring == 0 else 6 + ao * 6 + role
-        rows = pl.ds(slot_row(ao, bo, h), 160)
+        role = {3: 0, 1: 1, 2: 2}[offset] * PIECES + h
+        index = role if ring == 0 else 3 * PIECES * (1 + ao) + role
+        rows = pl.ds(slot_row(ao, bo, h), SLOT_PIECE)
         pltpu.make_async_remote_copy(
             src_ref=weights.at[rows, :],
             dst_ref=weights.at[rows, :],
@@ -236,8 +240,8 @@
         peer = (owner + k) % 8
         target_send[peer] = picked(teacher[...], peer)
     load_tokens.wait()
-    for h in range(2):
-        half = pl.ds(h * 160, 160)
+    def own_piece(h):
+        half = pl.ds(h * SLOT_PIECE, SLOT_PIECE)
         for k in (0, 4, 3, 5, 2, 6, 1, 7):
             source = (owner - k + 8) % 8
             table = unpack[pl.ds(pl.multiple_of(source * 256, 256), 256), :]
@@ -253,13 +257,10 @@
                 device_id_type=MESH,
             ).wait_recv()
             pre[half, :] += jnp.dot(weight_recv[source, half, :], table, preferred_element_type=F32)
-        weights[pl.ds(slot_row(0, 0, h), 160), :] = pre[half, :].astype(BF16)
+        weights[pl.ds(slot_row(0, 0, h), SLOT_PIECE), :] = pre[half, :].astype(BF16)
         for ring in (0, 1):
             for step in (1, 3):
                 ag_start(ring, step, 0, 0, h)
-        lax.fori_loop(h * 8, h * 8 + 8, norm, 0)
-    for k in (4, 3, 5, 2, 6, 1, 7):
-        target_copy(k).start()
 
     def chunk_copy(index, turn):
         return pltpu.make_async_remote_copy(
@@ -313,33 +314,58 @@
     def relay(ring, ao, bo, h):
         ag_wait(ring, ao, bo, h)
         far = ao if ring == 0 else bo
-        if far == 3 and h == 0:
+        if far == 3 and h < PIECES // 2:
             ag_start(ring, 1, ao, bo, h)
-        if far == 1 and h == 1:
+        if far == 1 and h >= PIECES // 2:
             ag_start(ring, 3, ao, bo, h)
         if ring == 0:
             ag_start(1, 1, ao, 0, h)
             ag_start(1, 3, ao, 0, h)
 
-    relay(0, 3, 0, 0)
-    relay(0, 1, 0, 0)
-    relay(1, 0, 3, 0)
-    fill(0, 2)
-    relay(0, 1, 0, 1)
-    relay(0, 3, 0, 1)
-    relay(1, 0, 1, 1)
-    fill(2, 4)
+    def first_relays(h):
+        near = 3 if h < PIECES // 2 else 1
+        relay(0, near, 0, h)
+        relay(0, 4 - near, 0, h)
+        relay(1, 0, near, h)
+
+    own_piece(0)
+    lax.fori_loop(0, 4, norm, 0)
+    own_piece(1)
+    first_relays(0)
+    lax.fori_loop(4, 8, norm, 0)
+    own_piece(2)
+    first_relays(1)
+    lax.fori_loop(8, 12, norm, 0)
+    own_piece(3)
+    for k in (4, 3, 5, 2, 6, 1, 7):
+        target_copy(k).start()
+    first_relays(2)
+    lax.fori_loop(12, 16, norm, 0)
+    first_relays(3)
+    fill(0, 1)
     relay(0, 2, 0, 0)
-    fill(4, 6)
     relay(0, 2, 0, 1)
+    fill(1, 2)
     relay(1, 3, 3, 0)
-    fill(6, 7)
-    relay(1, 3, 1, 1)
     relay(1, 1, 3, 0)
-    fill(7, 8)
-    relay(1, 1, 1, 1)
-    fill(8, 10)
+    fill(2, 3)
+    relay(0, 2, 0, 2)
+    relay(0, 2, 0, 3)
+    fill(3, 4)
+    relay(1, 3, 3, 1)
+    relay(1, 1, 3, 1)
+    fill(4, 5)
+    relay(1, 3, 1, 2)
+    relay(1, 1, 1, 2)
+    fill(5, 6)
+    relay(1, 3, 1, 3)
+    relay(1, 1, 1, 3)
+    fill(6, 8)
     relay(1, 2, 3, 0)
+    fill(8, 9)
+    relay(1, 2, 3, 1)
+    fill(9, 10)
+    relay(1, 2, 1, 2)
 
     @pl.loop(0, 16)
     def _(s):
@@ -347,7 +373,7 @@
         cols = pl.ds(pl.multiple_of((bb * 4 + aa + core * 3 * (aa - bb)) * 256, 256), 256)
         normed_t[pl.ds(pl.multiple_of(s * 256, 256), 256), :] = normed[:, cols].T
 
-    relay(1, 2, 1, 1)
+    relay(1, 2, 1, 3)
 
     for k in range(1, 8):
         source = (owner - k + 8) % 8
@@ -369,21 +395,30 @@
         target[:, cols] = total.astype(BF16)
 
     take_chunks(0, 10)
-    for bo, h in ((3, 1), (1, 0), (2, 0), (2, 1)):
-        ag_wait(1, 0, bo, h)
+    lower, upper = range(PIECES // 2), range(PIECES // 2, PIECES)
+
+    def group_waits(ao):
+        for h in upper:
+            ag_wait(1, ao, 3, h)
+        for h in lower:
+            ag_wait(1, ao, 1, h)
+        for h in range(PIECES):
+            ag_wait(1, ao, 2, h)
+
+    group_waits(0)
     multiply_group(0, True)
-    for ao in (3, 1, 2):
-        ag_wait(1, ao, 3, 1)
-    for h in range(2):
-        ag_wait(1, 3, 2, h)
-    ag_wait(1, 3, 1, 0)
+    group_waits(3)
+    for ao in (1, 2):
+        for h in upper:
+            ag_wait(1, ao, 3, h)
     multiply_group(3, False)
     for ao in (1, 2):
-        ag_wait(1, ao, 1, 0)
-    for h in range(2):
+        for h in lower:
+            ag_wait(1, ao, 1, h)
+    for h in range(PIECES):
         ag_wait(1, 1, 2, h)
     multiply_group(1, False)
-    for h in range(2):
+    for h in range(PIECES):
         ag_wait(1, 2, 2, h)
     multiply_group(2, False)
 
@@ -396,7 +431,7 @@
     for copy in ag_started:
         copy.wait_send()
     for k in range(1, 8):
-        for h in range(2):
+        for h in range(PIECES):
             weight_copy(k, h).wait_send()
         target_copy(k).wait_send()
 
@@ -408,13 +443,18 @@
 
     def grad_row(ao, bo, h):
         aa, bb = (a + ao) % 4, (b + bo) % 4
-        return pl.multiple_of((aa * 4 + bb) * 256 + h * 128, 128)
+        return pl.multiple_of((aa * 4 + bb) * 256 + h * GRAD_PIECE, GRAD_PIECE)
+
+    def landing(ring, ao, role):
+        index = role if ring == 0 else 3 * PIECES * (1 + ao) + role
+        place = ring_a if ring == 0 else ring_b
+        start = (role if ring == 0 else ao * 3 * PIECES + role) * GRAD_PIECE
+        return place.at[pl.ds(start, GRAD_PIECE), :], index
 
     def rs_start(ring, step, ao, bo, h, role):
-        index = role if ring == 0 else 6 + ao * 6 + role
-        place = ring_a.at[pl.ds(role * 128, 128), :] if ring == 0 else ring_b.at[pl.ds((ao * 6 + role) * 128, 128), :]
+        place, index = landing(ring, ao, role)
         copy = pltpu.make_async_remote_copy(
-            src_ref=weights.at[pl.ds(grad_row(ao, bo, h), 128), :],
+            src_ref=weights.at[pl.ds(grad_row(ao, bo, h), GRAD_PIECE), :],
             dst_ref=place,
             send_sem=rs_send.at[len(rs_started)],
             recv_sem=rs_recv.at[index],
@@ -425,8 +465,7 @@
         rs_started.append(copy)
 
     def rs_take(ring, ao, role):
-        index = role if ring == 0 else 6 + ao * 6 + role
-        place = ring_a.at[pl.ds(role * 128, 128), :] if ring == 0 else ring_b.at[pl.ds((ao * 6 + role) * 128, 128), :]
+        place, index = landing(ring, ao, role)
         pltpu.make_async_remote_copy(
             src_ref=place,
             dst_ref=place,
@@ -440,13 +479,13 @@
     def add_into(ao, bo, h, places_in, final=False):
         base = grad_row(ao, bo, h)
 
-        @pl.loop(0, 8)
+        @pl.loop(0, GRAD_PIECE // 16)
         def _(r):
             total = weights[pl.ds(base + r * 16, 16), :].astype(F32)
             for place in places_in:
                 total += place[pl.ds(pl.multiple_of(r * 16, 16), 16), :].astype(F32)
             if final:
-                out_ref[pl.ds(pl.multiple_of(h * 128 + r * 16, 16), 16), :] = total
+                out_ref[pl.ds(pl.multiple_of(h * GRAD_PIECE + r * 16, 16), 16), :] = total
             else:
                 weights[pl.ds(base + r * 16, 16), :] = total.astype(BF16)
 
@@ -461,24 +500,30 @@
                 normed_t[rows, :], delta[:, cols], preferred_element_type=F32
             ).astype(BF16)
 
+    left, right = PIECES, 2 * PIECES
+
     def spread_b(ao, only=None):
         if only in (None, 2):
-            rs_start(1, 1, ao, 2, 0, 0)
-            rs_start(1, 3, ao, 2, 1, 1)
+            for h in lower:
+                rs_start(1, 1, ao, 2, h, h)
+            for h in upper:
+                rs_start(1, 3, ao, 2, h, h)
         if only in (None, 1):
-            rs_start(1, 1, ao, 1, 1, 3)
+            for h in upper:
+                rs_start(1, 1, ao, 1, h, left + h)
         if only in (None, 3):
-            rs_start(1, 3, ao, 3, 0, 4)
+            for h in lower:
+                rs_start(1, 3, ao, 3, h, right + h)
 
     def relay_b(ao):
-        add_into(ao, 1, 0, [rs_take(1, ao, 0)])
-        rs_start(1, 1, ao, 1, 0, 2)
-        add_into(ao, 3, 1, [rs_take(1, ao, 1)])
-        rs_start(1, 3, ao, 3, 1, 5)
-
-    def gather_b(ao):
-        for h in range(2):
-            add_into(ao, 0, h, [rs_take(1, ao, 2 + h), rs_take(1, ao, 4 + h)])
+        for low, high in zip(lower, upper):
+            add_into(ao, 1, low, [rs_take(1, ao, low)])
+            rs_start(1, 1, ao, 1, low, left + low)
+            add_into(ao, 3, high, [rs_take(1, ao, high)])
+            rs_start(1, 3, ao, 3, high, right + high)
+
+    def gather_b(ao, h):
+        add_into(ao, 0, h, [rs_take(1, ao, left + h), rs_take(1, ao, right + h)])
 
     for bo in (2, 1, 3):
         products(2, bo, 1)
@@ -493,24 +538,27 @@
     products(0, 0, 4)
     spread_b(0)
     products(2, 0, 1)
-    gather_b(2)
-    rs_start(0, 1, 2, 0, 0, 0)
-    rs_start(0, 3, 2, 0, 1, 1)
-    gather_b(1)
-    rs_start(0, 1, 1, 0, 1, 3)
-    gather_b(3)
-    rs_start(0, 3, 3, 0, 0, 4)
-    add_into(1, 0, 0, [rs_take(0, 0, 0)])
-    rs_start(0, 1, 1, 0, 0, 2)
-    add_into(3, 0, 1, [rs_take(0, 0, 1)])
-    rs_start(0, 3, 3, 0, 1, 5)
+    for h in range(PIECES):
+        gather_b(2, h)
+        rs_start(0, 1 if h in lower else 3, 2, 0, h, h)
+    for h in upper:
+        gather_b(1, h)
+        rs_start(0, 1, 1, 0, h, left + h)
+    for h in lower:
+        gather_b(3, h)
+        rs_start(0, 3, 3, 0, h, right + h)
+    for h in lower:
+        gather_b(1, h)
+        add_into(1, 0, h, [rs_take(0, 0, h)])
+        rs_start(0, 1, 1, 0, h, left + h)
+    for h in upper:
+        gather_b(3, h)
+        add_into(3, 0, h, [rs_take(0, 0, h)])
+        rs_start(0, 3, 3, 0, h, right + h)
     relay_b(0)
-    for h in range(2):
-        add_into(
-            0, 0, h,
-            [rs_take(1, 0, 2 + h), rs_take(1, 0, 4 + h), rs_take(0, 0, 2 + h), rs_take(0, 0, 4 + h)],
-            final=True,
-        )
+    for h in range(PIECES):
+        places_in = [rs_take(ring, 0, side + h) for ring in (1, 0) for side in (left, right)]
+        add_into(0, 0, h, places_in, final=True)
     for copy in rs_started:
         copy.wait_send()
 
@@ -551,14 +599,14 @@
             pltpu.VMEM((1, 4096), F32),
             pltpu.VMEM((200, 128), jnp.int32),
             dma((3,)),
-            dma((16,)),
-            dma((16,)),
+            dma((8 * PIECES,)),
+            dma((8 * PIECES,)),
             dma((8,)),
             dma((8,)),
-            dma((30,)),
-            dma((30,)),
-            dma((30,)),
-            dma((30,)),
+            dma((15 * PIECES,)),
+            dma((15 * PIECES,)),
+            dma((15 * PIECES,)),
+            dma((15 * PIECES,)),
             dma((10,)),
             dma((10,)),
         ],

time: 129 us -> 134 us (1.039)
  Pallas kernels: 125 us -> 130 us
    pallas_call x1, Pallas kernels: 125 us -> 130 us  [per_device(): pl.pallas_call(body, out_shape=jax.ShapeDtypeStruct((256, 1024), F32), in...]
where the time goes in v6:
time: 134 us; the launch traced here: 132 us
  Pallas kernels  130 us (97%)
  local copies, waits for them, and re-layouts  2.31 us (2%)
    pallas_call x1, Pallas kernels, per_device(): pl.pallas_call(body, out_shape=jax.ShapeDtypeStruct((256, 1024), F32), in...  130 us

profile of v6, /device:TPU:34, one launch (start us, length us, event | category | flops | bytes accessed | tf_op | source)
XLA Modules:
  0.0 131.9 jit_solution(16556201323457656604)
XLA Ops:
  0.0 129.6 %shard_map.64 = f32[256,1024]{1,0:T(8,128)} custom-call(bf16[512,4096]{1,0:T(8,128)(2,1)} %refs_0_.1, bf16[512,1536]{1,0:T(8,128)(2,1)} %refs_1_.1, bf16[384,1536]{1,0:T(8,128)(2,1)} %refs_2_.1, f32[48,128]{1,0:T(8,128)} %bitcast.4, s32[32,128]{1,0:T(8,128)} %bitcast.5, s32[64,128]{1,0:T(8,128)} %bitcast.3), custom_call_target="tpu_custom_call" | custom-call | flops 40000000000 | bytes 10000000 | tf_op jit(solution)/shard_map/pallas_call | solution.py:575
  129.6 2.3 %copy.8 = f32[256,1024]{1,0:T(8,128)} copy(f32[256,1024]{1,0:T(8,128)} %shard_map.64) | data formatting | bytes 2097152

commit v7 on v6

--- a/solution.py
+++ b/solution.py
@@ -10,7 +10,7 @@
 MESH = pl.DeviceIdType.MESH
 SLOT_ROWS = 320
 SLOT_COLS = 256
-PIECES = 4
+PIECES = 2
 SLOT_PIECE = SLOT_ROWS // PIECES
 GRAD_PIECE = 256 // PIECES
 BF16 = jnp.bfloat16
@@ -46,6 +46,7 @@
     normed, normed_t, packed_x, weights, teacher, up, kept_rows, weight_send, weight_recv,
     target_send, target_recv, unpack, picks, pre, delta, target, ring_b, ring_a, gain, places,
     local_sems, ws_send, ws_recv, ts_send, ts_recv, ag_send, ag_recv, rs_send, rs_recv, px_send, px_recv,
+    hops, hop_send, hop_recv, onward_send,
 ):
     dp = lax.axis_index("dp")
     owner = lax.axis_index("tensor")
@@ -141,20 +142,49 @@
 
     pl.semaphore_wait(barrier, 11)
 
-    def pack(i, carry):
-        k = 4 + (i + 1) // 2 * (1 - 2 * (i % 2))
+    near, beyond = 3 + 2 * core, 5 - 2 * core
+
+    def hop_copy(way, j):
+        peer = (owner + (4 if j == 0 else beyond)) % 8
+        return pltpu.make_async_remote_copy(
+            src_ref=weight_send.at[peer, pl.ds(way * SLOT_PIECE, SLOT_PIECE), :],
+            dst_ref=hops.at[2 * way + j],
+            send_sem=hop_send.at[2 * way + j],
+            recv_sem=hop_recv.at[2 * way + j],
+            device_id=(dp, (owner + (2 if way == 0 else 6)) % 8),
+            device_id_type=MESH,
+        )
+
+    def onward_copy(way, j):
+        origin = (owner + (6 if way == 0 else 2)) % 8
+        k = 4 if j == 0 else beyond
+        return pltpu.make_async_remote_copy(
+            src_ref=hops.at[2 * way + j],
+            dst_ref=weight_recv.at[origin, pl.ds(way * SLOT_PIECE, SLOT_PIECE), :],
+            send_sem=onward_send.at[2 * way + j],
+            recv_sem=ws_recv.at[way * 8 + k],
+            device_id=(dp, (origin + k) % 8),
+            device_id_type=MESH,
+        )
+
+    def pack(k):
         peer = (owner + k) % 8
-        make_pick(peer, carry)
+        make_pick(peer, 0)
         weight_send[peer] = picked(kept_rows[...], peer)
+
+    for j in range(2):
+        pack(beyond if j == 1 else 4)
+        for way in range(2):
+            hop_copy(way, j).start()
+    for k in (2, 6, near):
+        pack(k)
         weight_copy(k, 0).start()
-        return carry
-
-    lax.fori_loop(0, 7, pack, 0)
-    for h in range(1, PIECES):
-        for k in (4, 3, 5, 2, 6, 1, 7):
-            weight_copy(k, h).start()
-    make_pick(owner, 0)
-    weight_send[owner] = picked(kept_rows[...], owner)
+    for k in (1, 7):
+        pack(k)
+        weight_copy(k, 0).start()
+    for k in (2, 6, near, 1, 7):
+        weight_copy(k, 1).start()
+    pack(0)
 
     own = ff_ref[pl.ds(pl.multiple_of(owner * 8, 8), 8), :]
     source = blocks_of(own, 1536, 8)
@@ -234,6 +264,10 @@
             device_id_type=MESH,
         ).wait_recv()
 
+    for way in range(2):
+        for j in range(2):
+            hop_copy(way, j).wait_recv()
+            onward_copy(way, j).start()
     load_teacher.wait()
     target_recv[owner] = picked(teacher[...], owner)
     for k in (4, 3, 5, 2, 6, 1, 7):
@@ -242,7 +276,7 @@
     load_tokens.wait()
     def own_piece(h):
         half = pl.ds(h * SLOT_PIECE, SLOT_PIECE)
-        for k in (0, 4, 3, 5, 2, 6, 1, 7):
+        for k in (0, 1, 7, 2, 6, 3, 5, 4):
             source = (owner - k + 8) % 8
             table = unpack[pl.ds(pl.multiple_of(source * 256, 256), 256), :]
             if k == 0:
@@ -323,49 +357,32 @@
             ag_start(1, 3, ao, 0, h)
 
     def first_relays(h):
-        near = 3 if h < PIECES // 2 else 1
-        relay(0, near, 0, h)
-        relay(0, 4 - near, 0, h)
-        relay(1, 0, near, h)
+        side = 3 if h < PIECES // 2 else 1
+        relay(0, side, 0, h)
+        relay(0, 4 - side, 0, h)
+        relay(1, 0, side, h)
 
     own_piece(0)
-    lax.fori_loop(0, 4, norm, 0)
+    lax.fori_loop(0, 8, norm, 0)
+    first_relays(0)
     own_piece(1)
-    first_relays(0)
-    lax.fori_loop(4, 8, norm, 0)
-    own_piece(2)
-    first_relays(1)
-    lax.fori_loop(8, 12, norm, 0)
-    own_piece(3)
     for k in (4, 3, 5, 2, 6, 1, 7):
         target_copy(k).start()
-    first_relays(2)
-    lax.fori_loop(12, 16, norm, 0)
-    first_relays(3)
+    lax.fori_loop(8, 16, norm, 0)
+    first_relays(1)
     fill(0, 1)
     relay(0, 2, 0, 0)
-    relay(0, 2, 0, 1)
     fill(1, 2)
     relay(1, 3, 3, 0)
     relay(1, 1, 3, 0)
     fill(2, 3)
-    relay(0, 2, 0, 2)
-    relay(0, 2, 0, 3)
+    relay(0, 2, 0, 1)
     fill(3, 4)
-    relay(1, 3, 3, 1)
-    relay(1, 1, 3, 1)
-    fill(4, 5)
-    relay(1, 3, 1, 2)
-    relay(1, 1, 1, 2)
-    fill(5, 6)
-    relay(1, 3, 1, 3)
-    relay(1, 1, 1, 3)
-    fill(6, 8)
+    relay(1, 3, 1, 1)
+    relay(1, 1, 1, 1)
+    fill(4, 7)
     relay(1, 2, 3, 0)
-    fill(8, 9)
-    relay(1, 2, 3, 1)
-    fill(9, 10)
-    relay(1, 2, 1, 2)
+    fill(7, 9)
 
     @pl.loop(0, 16)
     def _(s):
@@ -373,7 +390,8 @@
         cols = pl.ds(pl.multiple_of((bb * 4 + aa + core * 3 * (aa - bb)) * 256, 256), 256)
         normed_t[pl.ds(pl.multiple_of(s * 256, 256), 256), :] = normed[:, cols].T
 
-    relay(1, 2, 1, 3)
+    relay(1, 2, 1, 1)
+    fill(9, 10)
 
     for k in range(1, 8):
         source = (owner - k + 8) % 8
@@ -431,9 +449,14 @@
     for copy in ag_started:
         copy.wait_send()
     for k in range(1, 8):
+        target_copy(k).wait_send()
+    for k in (2, 6, near, 1, 7):
         for h in range(PIECES):
             weight_copy(k, h).wait_send()
-        target_copy(k).wait_send()
+    for way in range(2):
+        for j in range(2):
+            hop_copy(way, j).wait_send()
+            onward_copy(way, j).wait_send()
 
     @pl.loop(0, 10)
     def _(turn):
@@ -609,6 +632,10 @@
             dma((15 * PIECES,)),
             dma((10,)),
             dma((10,)),
+            pltpu.VMEM((4, SLOT_PIECE, SLOT_COLS), BF16),
+            dma((4,)),
+            dma((4,)),
+            dma((4,)),
         ],
         compiler_params=pltpu.CompilerParams(
             collective_id=0, has_side_effects=True, vmem_limit_bytes=62 * 1024 * 1024

time: 134 us -> 138 us (1.030)
  the two profiles are of different devices: /device:TPU:34 before, /device:TPU:0 now
where the time goes in v7:
time: 138 us
  Pallas kernels  135 us (98%)
  local copies, waits for them, and re-layouts  2.31 us (2%)
    pallas_call x1, Pallas kernels, per_device(): pl.pallas_call(body, out_shape=jax.ShapeDtypeStruct((256, 1024), F32), in...  135 us

profile of v7, /device:TPU:0, one launch (start us, length us, event | category | flops | bytes accessed | tf_op | source)
XLA Modules:
  0.0 137.6 jit_solution(2754566314674533082)
XLA Ops:
  0.0 135.3 %shard_map.64 = f32[256,1024]{1,0:T(8,128)} custom-call(bf16[512,4096]{1,0:T(8,128)(2,1)} %refs_0_.1, bf16[512,1536]{1,0:T(8,128)(2,1)} %refs_1_.1, bf16[384,1536]{1,0:T(8,128)(2,1)} %refs_2_.1, f32[48,128]{1,0:T(8,128)} %bitcast.4, s32[32,128]{1,0:T(8,128)} %bitcast.5, s32[64,128]{1,0:T(8,128)} %bitcast.3), custom_call_target="tpu_custom_call" | custom-call | flops 40000000000 | bytes 10000000 | tf_op jit(solution)/shard_map/pallas_call | solution.py:598
  135.3 2.3 %copy.8 = f32[256,1024]{1,0:T(8,128)} copy(f32[256,1024]{1,0:T(8,128)} %shard_map.64) | data formatting | bytes 2097152

commit v8 on v5

--- a/solution.py
+++ b/solution.py
@@ -147,8 +147,6 @@
         return carry
 
     lax.fori_loop(0, 7, pack, 0)
-    for k in (4, 3, 5, 2, 6, 1, 7):
-        weight_copy(k, 1).start()
     make_pick(owner, 0)
     weight_send[owner] = picked(kept_rows[...], owner)
 
@@ -230,6 +228,10 @@
             device_id_type=MESH,
         ).wait_recv()
 
+    for k in (4, 3, 5, 2, 6, 1, 7):
+        weight_copy(k, 0).wait_send()
+    for k in (4, 3, 5, 2, 6, 1, 7):
+        weight_copy(k, 1).start()
     load_teacher.wait()
     target_recv[owner] = picked(teacher[...], owner)
     for k in (4, 3, 5, 2, 6, 1, 7):
@@ -298,16 +300,17 @@
         def _(turn):
             chunk_copy((z * 5 + 2 * turn + 1 - core) % 20, turn).wait_recv()
 
-    def multiply_group(zo, first):
+    def multiply_group(zo, first, start=0, count=5):
         base = ((z + zo) % 4) * 5
 
         @pl.loop(0, 2)
         def _(n):
             cols = pl.ds(pl.multiple_of(n * 512, 512), 512)
             part = jnp.zeros((512, 512), F32) if first else pre[:, cols]
-            for c in range(5):
-                depth = pl.ds(pl.multiple_of((base + c) * 256, 256), 256)
-                part += jnp.dot(packed_x[base + c], weights[depth, cols], preferred_element_type=F32)
+            for c in range(count):
+                chunk = base + (start + c) % 5
+                depth = pl.ds(pl.multiple_of(chunk * 256, 256), 256)
+                part += jnp.dot(packed_x[chunk], weights[depth, cols], preferred_element_type=F32)
             pre[:, cols] = part
 
     def relay(ring, ao, bo, h):
@@ -383,9 +386,11 @@
     for h in range(2):
         ag_wait(1, 1, 2, h)
     multiply_group(1, False)
+    late = (x + 2) % 4
+    multiply_group(2, False, late + 2, 3)
     for h in range(2):
         ag_wait(1, 2, 2, h)
-    multiply_group(2, False)
+    multiply_group(2, False, late, 2)
 
     @pl.loop(0, 32)
     def _(r):
@@ -396,8 +401,7 @@
     for copy in ag_started:
         copy.wait_send()
     for k in range(1, 8):
-        for h in range(2):
-            weight_copy(k, h).wait_send()
+        weight_copy(k, 1).wait_send()
         target_copy(k).wait_send()
 
     @pl.loop(0, 10)
@@ -485,17 +489,17 @@
         spread_b(2, bo)
     products(1, 0, 4)
     spread_b(1)
+    relay_b(2)
     products(3, 0, 4)
     spread_b(3)
-    relay_b(2)
     relay_b(1)
-    relay_b(3)
-    products(0, 0, 4)
-    spread_b(0)
     products(2, 0, 1)
     gather_b(2)
     rs_start(0, 1, 2, 0, 0, 0)
     rs_start(0, 3, 2, 0, 1, 1)
+    products(0, 0, 4)
+    relay_b(3)
+    spread_b(0)
     gather_b(1)
     rs_start(0, 1, 1, 0, 1, 3)
     gather_b(3)

time: 129 us -> 128 us (level)
  no operation moved by 1% of the time
where the time goes in v8:
time: 128 us; the launch traced here: 127 us
  Pallas kernels  125 us (98%)
  local copies, waits for them, and re-layouts  2.31 us (2%)
    pallas_call x1, Pallas kernels, per_device(): pl.pallas_call(body, out_shape=jax.ShapeDtypeStruct((256, 1024), F32), in...  125 us

profile of v8, /device:TPU:34, one launch (start us, length us, event | category | flops | bytes accessed | tf_op | source)
XLA Modules:
  0.0 126.9 jit_solution(1419409882906531713)
XLA Ops:
  0.0 124.6 %shard_map.64 = f32[256,1024]{1,0:T(8,128)} custom-call(bf16[512,4096]{1,0:T(8,128)(2,1)} %refs_0_.1, bf16[512,1536]{1,0:T(8,128)(2,1)} %refs_1_.1, bf16[384,1536]{1,0:T(8,128)(2,1)} %refs_2_.1, f32[48,128]{1,0:T(8,128)} %bitcast.4, s32[32,128]{1,0:T(8,128)} %bitcast.5, s32[64,128]{1,0:T(8,128)} %bitcast.3), custom_call_target="tpu_custom_call" | custom-call | flops 40000000000 | bytes 10000000 | tf_op jit(solution)/shard_map/pallas_call | solution.py:531
  124.6 2.3 %copy.8 = f32[256,1024]{1,0:T(8,128)} copy(f32[256,1024]{1,0:T(8,128)} %shard_map.64) | data formatting | bytes 2097152

commit v9 on v8

--- a/solution.py
+++ b/solution.py
@@ -388,6 +388,8 @@
     multiply_group(1, False)
     late = (x + 2) % 4
     multiply_group(2, False, late + 2, 3)
+    for copy in ag_started[:24]:
+        copy.wait_send()
     for h in range(2):
         ag_wait(1, 2, 2, h)
     multiply_group(2, False, late, 2)
@@ -398,15 +400,8 @@
         active = jnp.maximum(pre[rows, :], 0.0)
         delta[rows, :] = (2.0 * active * (active * active - target[rows, :].astype(F32)) * scale).astype(BF16)
 
-    for copy in ag_started:
+    for copy in ag_started[24:]:
         copy.wait_send()
-    for k in range(1, 8):
-        weight_copy(k, 1).wait_send()
-        target_copy(k).wait_send()
-
-    @pl.loop(0, 10)
-    def _(turn):
-        chunk_copy((z * 5 + 2 * turn + core) % 20, turn).wait_send()
 
     rs_started = []
 
@@ -517,6 +512,13 @@
         )
     for copy in rs_started:
         copy.wait_send()
+    for k in range(1, 8):
+        weight_copy(k, 1).wait_send()
+        target_copy(k).wait_send()
+
+    @pl.loop(0, 10)
+    def _(turn):
+        chunk_copy((z * 5 + 2 * turn + core) % 20, turn).wait_send()
 
 
 def per_device(tokens_in, teacher_hidden, up_old, gain_old, keep_chan, keep_ff):

time: 128 us -> 128 us (level)
  no operation moved by 1% of the time
where the time goes in v9:
time: 128 us; the launch traced here: 127 us
  Pallas kernels  125 us (98%)
  local copies, waits for them, and re-layouts  2.31 us (2%)
    pallas_call x1, Pallas kernels, per_device(): pl.pallas_call(body, out_shape=jax.ShapeDtypeStruct((256, 1024), F32), in...  125 us

profile of v9, /device:TPU:34, one launch (start us, length us, event | category | flops | bytes accessed | tf_op | source)
XLA Modules:
  0.0 126.8 jit_solution(6380986739701192329)
XLA Ops:
  0.0 124.5 %shard_map.64 = f32[256,1024]{1,0:T(8,128)} custom-call(bf16[512,4096]{1,0:T(8,128)(2,1)} %refs_0_.1, bf16[512,1536]{1,0:T(8,128)(2,1)} %refs_1_.1, bf16[384,1536]{1,0:T(8,128)(2,1)} %refs_2_.1, f32[48,128]{1,0:T(8,128)} %bitcast.4, s32[32,128]{1,0:T(8,128)} %bitcast.5, s32[64,128]{1,0:T(8,128)} %bitcast.3), custom_call_target="tpu_custom_call" | custom-call | flops 40000000000 | bytes 10000000 | tf_op jit(solution)/shard_map/pallas_call | solution.py:533
  124.5 2.3 %copy.8 = f32[256,1024]{1,0:T(8,128)} copy(f32[256,1024]{1,0:T(8,128)} %shard_map.64) | data formatting | bytes 2097152
